TPU v7x, 256 devices: a whole 4x4x8 slice. The times are simulated.
256 devices in a mesh: src: 16 (over y, z_lo), tgt: 16 (over z_hi, x, core).
Axes of the slice: x: 4, y: 4, z: 8 (z_hi: 2, z_lo: 4; z = z_hi * 4 + z_lo), core: 2. Of those that a mesh axis runs over, the one named last changes fastest.
Arguments:
- edge_state: bfloat16 [16, 16, 1024, 512], P('src', 'tgt'), may hold values from -6 to 6
- edge_source: int32 [16, 16, 1024], P('src', 'tgt'), may hold values from 0 to 1023
- edge_target: int32 [16, 16, 1024], P('src', 'tgt'), may hold values from 0 to 1023
- live_edges: int32 [16, 16], P('src', 'tgt'), may hold values from 64 to 1024, as said below
- inner_one: bfloat16 [512, 512], replicated, may hold values from -0.25 to 0.25
- outer_one: bfloat16 [512, 512], replicated, may hold values from -0.25 to 0.25
- inner_two: bfloat16 [512, 512], replicated, may hold values from -0.25 to 0.25
- outer_two: bfloat16 [512, 512], replicated, may hold values from -0.25 to 0.25
- gain_one: float32 [512], replicated, may hold values from 0.1 to 1.9
- gain_two: float32 [512], replicated, may hold values from 0.1 to 1.9
Outputs:
- final_state: bfloat16 [16, 16, 1024, 512], P('src', 'tgt')
Inputs may be any that keep to these rules, and one draw needn't show every extreme that they name: `edge_source`: source atoms within a block. `edge_target`: target atoms within a block. `live_edges`: a multiple of 64; some block pair is full in every draw.
All inputs are finite; a program needn't handle non-finite values.
Results may differ from a plain program's by a relative error of at most 0.013.
Values sent between devices are 32-bit elements; how exact they have to be, the bound alone decides.
A program may use at most 64 MiB of HBM per device.

v0:
```python
import jax
import jax.numpy as jnp
from jax import lax
from jax.sharding import PartitionSpec as P

ATOM_DEV = 64


def update_edges(message, inner, outer, gain):
    mean_square = jnp.mean(message * message, axis=-1, keepdims=True)
    normed = message * lax.rsqrt(mean_square + 1e-05) * gain
    normed_low = normed.astype(jnp.bfloat16)
    activated = jax.nn.relu(jnp.dot(normed_low, inner, preferred_element_type=jnp.float32)).astype(
        jnp.bfloat16
    )
    return normed + jnp.dot(activated, outer, preferred_element_type=jnp.float32)


def apply_layer(message, alive, inner, outer, gain):
    result = update_edges(message, inner, outer, gain)
    return jnp.where(alive[:, None], result, jnp.float32(0.0)).astype(jnp.bfloat16)


def target_totals(partial_value):
    return lax.psum(partial_value, "src")


def source_totals(partial_value):
    return lax.psum(partial_value, "tgt")


def body(
    edge_state,
    edge_source,
    edge_target,
    live_edges,
    inner_one,
    outer_one,
    inner_two,
    outer_two,
    gain_one,
    gain_two,
):
    edge_rows = edge_state.shape[2]
    channels = edge_state.shape[3]
    states = edge_state.reshape(edge_rows, channels)
    sources = edge_source.reshape(edge_rows)
    targets = edge_target.reshape(edge_rows)
    live_count = live_edges.reshape(())
    alive = lax.iota(jnp.int32, edge_rows) < live_count
    target_group = ATOM_DEV * lax.axis_size("src")
    source_group = ATOM_DEV * lax.axis_size("tgt")
    partial_value = jax.ops.segment_sum(
        jnp.where(alive[:, None], states.astype(jnp.float32), jnp.float32(0.0)),
        targets,
        num_segments=target_group,
    )
    incoming = target_totals(partial_value)
    message = jnp.take(incoming, targets, axis=0) - states.astype(jnp.float32)
    reverse_state = apply_layer(message, alive, inner_one, outer_one, gain_one)
    reverse_wide = reverse_state.astype(jnp.float32)
    partial_two = jax.ops.segment_sum(reverse_wide, sources, num_segments=source_group)
    outgoing = source_totals(partial_two)
    message_two = jnp.take(outgoing, sources, axis=0) - reverse_wide
    final_state = apply_layer(message_two, alive, inner_two, outer_two, gain_two)
    return final_state.reshape(1, 1, edge_rows, channels)


def solution(mesh):
    placed = (
        P("src", "tgt", None, None),
        P("src", "tgt", None),
        P("src", "tgt", None),
        P("src", "tgt"),
        P(),
        P(),
        P(),
        P(),
        P(),
        P(),
    )
    return jax.shard_map(
        body, mesh=mesh, in_specs=placed, out_specs=P("src", "tgt", None, None), check_vma=False
    )
```

profile of v0, /device:TPU:1, one launch (start us, length us, event | category | flops | bytes accessed | tf_op | source)
XLA Modules:
  0.0 435.1 jit_solution(15807752797027591494)
XLA Ops:
  6.5 0.0 copy-start
  6.5 0.0 all-reduce.3.cloned.1.call-start
  6.5 1.5 copy.18
  8.7 1.6 convert_select_fusion
  10.3 0.0 copy-start.2
  10.3 3.0 copy.20
  13.3 0.0 copy-done.2
  13.3 8.6 %scatter_custom_fusion = f32[1024,512]{1,0:T(8,128)} fusion(s32[1024]{0:T(1024)S(1)} %bitcast.19, f32[1024,512]{1,0:T(8,128)} %copy.20, f32[]{:T(128)} %constant.4.clone.1), kind=kCustom, calls=%fused_computation.19 | custom fusion | flops 524288 | bytes 2097664 | tf_op jit(solution)/shard_map/scatter-add | solution.py:53
  21.9 0.0 all-reduce.3.cloned.1.call-update
  21.9 0.0 all-reduce.5.cloned.1.call-start
  22.0 170.6 %all-reduce.3.cloned.1.call-done = f32[1024,512]{1,0:T(8,128)} async-done(((f32[1024,512]{1,0:T(8,128)}), f32[1024,512]{1,0:T(8,128)}) %all-reduce.3.cloned.1.call-update) | async-done | bytes 2097168 | tf_op jit(solution)/shard_map/psum | solution.py:25
  192.6 6.9 %gather_fusion = f32[1024,512]{1,0:T(8,128)} fusion(f32[1024,512]{1,0:T(8,128)} %all-reduce.3.cloned.1.call-done, s32[1024]{0:T(1024)S(1)} %fusion.28), kind=kCustom, calls=%fused_computation.clone | custom fusion | bytes 4198400 | tf_op jit(solution)/shard_map/jit(_take)/gather | solution.py:59
  199.5 2.9 copy.21
  202.4 0.0 copy-start.4
  202.4 2.0 multiply_reduce_fusion.1
  204.5 0.0 copy-done
  204.5 0.0 copy-done.4
  204.5 0.0 copy-done.6
  204.5 5.2 %fusion.2 = f32[1024,512]{0,1:T(8,128)} fusion(bf16[512,512]{1,0:T(8,128)(2,1)S(1)} %copy-done, bf16[512,512]{1,0:T(8,128)(2,1)S(1)} %copy-done.4, f32[1024,512]{0,1:T(8,128)} %copy.21, bf16[1,1,1024,512]{2,3,1,0:T(8,128)(2,1)S(1)} %copy.18, f32[512]{0:T(512)S(1)} %copy-done.6, f32[1024]{0:T(1024)S(1)} %add_rsqrt_fusion.1, ...), kind=kOutput, calls=%fused_computation.17 | convolution fusion | flops 1082654720 | bytes 6299648 | tf_op jit(solution)/shard_map/dot_general | solution.py:16
  209.7 1.9 copy.23
  211.6 0.0 copy-done.3
  211.6 8.0 %scatter_custom_fusion.1 = f32[1024,512]{1,0:T(8,128)} fusion(s32[1024]{0:T(1024)S(1)} %bitcast.22, f32[1024,512]{1,0:T(8,128)S(1)} %copy.23, f32[]{:T(128)} %constant.4.clone.1), kind=kCustom, calls=%fused_computation.21 | custom fusion | flops 524288 | bytes 2097156 | tf_op jit(solution)/shard_map/scatter-add | solution.py:62
  219.6 0.0 all-reduce.5.cloned.1.call-update
  219.7 191.0 %all-reduce.5.cloned.1.call-done = f32[1024,512]{1,0:T(8,128)} async-done(((f32[1024,512]{1,0:T(8,128)}), f32[1024,512]{1,0:T(8,128)}) %all-reduce.5.cloned.1.call-update) | async-done | bytes 2097168 | tf_op jit(solution)/shard_map/psum | solution.py:29
  410.7 5.6 %gather_fusion.1 = f32[1024,512]{1,0:T(8,128)S(1)} fusion(f32[1024,512]{1,0:T(8,128)} %all-reduce.5.cloned.1.call-done, s32[1024]{0:T(1024)S(1)} %fusion.29), kind=kCustom, calls=%fused_computation.1.clone | custom fusion | bytes 4198400 | tf_op jit(solution)/shard_map/jit(_take)/gather | solution.py:64
  416.3 1.8 copy.24
  418.1 2.7 multiply_reduce_fusion
  420.8 0.1 copy-done.1
  421.0 0.1 copy-done.5
  421.0 0.0 copy-done.7
  421.0 4.9 %fusion.3 = bf16[1,1,1024,512]{2,3,1,0:T(8,128)(2,1)} fusion(bf16[512,512]{1,0:T(8,128)(2,1)S(1)} %copy-done.5, bf16[512,512]{1,0:T(8,128)(2,1)} %param.18, f32[512]{0:T(512)S(1)} %copy-done.7, f32[1024]{0:T(1024)S(1)} %add_rsqrt_fusion, pred[1024]{0:T(1024)(128)(4,1)S(1)} %iota_compare_fusion, f32[1024,512]{0,1:T(8,128)S(1)} %copy-done.1, ...), kind=kOutput, calls=%fused_computation.18 | convolution fusion | flops 1081081856 | bytes 6299648 | tf_op jit(solution)/shard_map/dot_general | solution.py:16
  425.9 2.3 copy.26
  (12 shorter events, 0.1 us)
Async XLA Ops:
  6.5 198.0 %copy-start = (bf16[512,512]{1,0:T(8,128)(2,1)S(1)}, bf16[512,512]{1,0:T(8,128)(2,1)}, u32[]{:S(2)}) copy-start(bf16[512,512]{1,0:T(8,128)(2,1)} %param.17) | copy-start | bytes 1572868
  6.5 186.1 %all-reduce.3.cloned.1.call-start = ((), (), s32[]{:S(2)}) async-start(), calls=%async_computation | async-start | bytes 4194304 | tf_op jit(solution)/shard_map/psum | solution.py:25
  10.3 3.0 copy-start.2
  21.9 388.7 %all-reduce.5.cloned.1.call-start = ((), (), s32[]{:S(2)}) async-start(), calls=%async_computation.1 | async-start | bytes 4194304 | tf_op jit(solution)/shard_map/psum | solution.py:29
  202.4 2.1 copy-start.4
  202.4 2.1 copy-start.6
  209.7 1.9 copy-start.3
  418.1 2.9 copy-start.1
  418.1 2.9 copy-start.5
  418.1 2.9 copy-start.7
Sparse Core Ops, SparseCore 0:
  22.1 170.5 all-reduce.2
  219.8 190.8 all-reduce.4
where the time goes:
time: 435 us
  waiting for transfers between devices  362 us (83%)
  local copies, waits for them, and re-layouts  26.2 us (6%)
  other arithmetic  23 us (5%)
  between operations  14.1 us (3%)
  matrix products  10.1 us (2%)
    psum x1, waiting for transfers between devices, source_totals(): return lax.psum(partial_value, 'tgt')  191 us
    psum x1, waiting for transfers between devices, target_totals(): return lax.psum(partial_value, 'src')  171 us
    dot_general x2, matrix products, update_edges(): jnp.dot(activated, outer, preferred_element_type=jnp.float32)  10.1 us
    gather x2, local copies, waits for them, and re-layouts, body(): message = jnp.take(incoming, targets, axis=0) - states.astype(jnp.float32)  9.84 us
  transfers between devices with their start and end apart: 2, of which 2 were waited for; matrix products, arithmetic and copies ran while one was open for 0% of the time, Pallas kernels for 0%

commit v1 on v0

v1 whole, which is shorter than its diff:
```python
import functools

import jax
import jax.numpy as jnp
from jax import lax
from jax.experimental import pallas as pl
from jax.experimental.pallas import tpu as pltpu
from jax.sharding import PartitionSpec as P

MESH = pl.DeviceIdType.MESH
CHUNKS = 4
RING = 4
TILE = 256
BF16 = jnp.bfloat16
F32 = jnp.float32


class Copies:
    def __init__(self, send_sems, recv_sems):
        self.send_sems, self.recv_sems = send_sems, recv_sems
        self.made = []

    def start(self, src, dst, device):
        i = len(self.made)
        copy = pltpu.make_async_remote_copy(
            src_ref=src,
            dst_ref=dst,
            send_sem=self.send_sems.at[i],
            recv_sem=self.recv_sems.at[i],
            device_id=device,
            device_id_type=MESH,
        )
        copy.start()
        self.made.append(copy)
        return copy


def rows_at(offset, count):
    return pl.ds(pl.multiple_of(offset, count), count)


class Ring:
    def __init__(self, copies, me, after, before, base, half, relay, direct, second):
        self.copies, self.me, self.after, self.before = copies, me, after, before
        self.base, self.half = base, half
        self.relay, self.direct, self.second = relay, direct, second

    def at(self, step, part):
        shard = (self.me + step + RING) % RING
        return rows_at(self.base + shard * (2 * self.half) + part * self.half, self.half)

    def reduce_first(self, data):
        start = self.copies.start
        self.relays = [
            start(data.at[self.at(2, 0)], self.relay.at[0], self.after),
            start(data.at[self.at(2, 1)], self.relay.at[1], self.before),
        ]
        self.directs = [
            start(data.at[self.at(1, 1)], self.direct.at[0], self.after),
            start(data.at[self.at(-1, 0)], self.direct.at[1], self.before),
        ]

    def reduce_second(self, data):
        start = self.copies.start
        self.seconds = []
        for way, (step, device) in enumerate(((1, self.after), (-1, self.before))):
            self.relays[way].wait_recv()
            rows = self.at(step, way)
            data[rows] = data[rows] + self.relay[way]
            self.seconds.append(start(data.at[rows], self.second.at[way], device))

    def reduce_last(self, data):
        for copy in self.directs + self.seconds:
            copy.wait_recv()
        low = data[self.at(0, 0)] + self.second[0] + self.direct[1]
        high = data[self.at(0, 1)] + self.direct[0] + self.second[1]
        return low, high

    def gather_first(self, full):
        start = self.copies.start
        low, high = self.at(0, 0), self.at(0, 1)
        self.firsts = [
            start(full.at[low], full.at[low], self.after),
            start(full.at[high], full.at[high], self.before),
        ]
        self.others = [
            start(full.at[high], full.at[high], self.after),
            start(full.at[low], full.at[low], self.before),
        ]

    def gather_second(self, full):
        start = self.copies.start
        for way, (step, device) in enumerate(((-1, self.after), (1, self.before))):
            self.firsts[way].wait_recv()
            rows = self.at(step, way)
            self.others.append(start(full.at[rows], full.at[rows], device))

    def gather_last(self):
        for copy in self.others:
            copy.wait_recv()


def kernel(
    state_ref,
    source_ref,
    target_ref,
    live_ref,
    inner_one_ref,
    outer_one_ref,
    inner_two_ref,
    outer_two_ref,
    gain_one_ref,
    gain_two_ref,
    out_ref,
    part_one,
    part_two,
    full_one,
    full_two,
    message,
    reverse,
    high,
    low,
    column_one,
    column_two,
    relay_one,
    direct_one,
    second_one,
    shard_one,
    cross_one,
    relay_two,
    direct_two,
    second_two,
    pair_two,
    cross_two,
    send_sems,
    recv_sems,
):
    rows, channels = state_ref.shape
    atoms = part_one.shape[0]
    chunk = atoms // CHUNKS

    src, tgt = lax.axis_index("src"), lax.axis_index("tgt")
    y, z_lo = src // 4, src % 4
    z_hi, x, core = tgt // 8, (tgt // 2) % 4, tgt % 2
    y_after, y_before = (((y + 1) % 4) * 4 + z_lo, tgt), (((y + 3) % 4) * 4 + z_lo, tgt)
    parity = z_lo % 2
    z_near, z_far = (y * 4 + z_lo + 1 - 2 * parity, tgt), (y * 4 + (z_lo + 2) % 4, tgt)
    sibling = (src, tgt + 1 - 2 * core)
    x_after = (src, z_hi * 8 + ((x + 1) % 4) * 2 + core)
    x_before = (src, z_hi * 8 + ((x + 3) % 4) * 2 + core)
    z_across = (src, (1 - z_hi) * 8 + x * 2 + core)

    barrier = pltpu.get_barrier_semaphore()
    partners = (y_after, y_before, z_near, z_far, sibling, x_after, x_before, z_across)
    for device in partners:
        pl.semaphore_signal(barrier, inc=1, device_id=device, device_id_type=MESH)

    live = live_ref[0, 0]
    alive = lax.broadcasted_iota(jnp.int32, (1, rows), 1) < live
    target_row = jnp.where(alive, target_ref[...], -1)
    source_row = jnp.where(alive, source_ref[...], -1)

    def scatter(part, values_ref, index_row, k):
        atom = lax.broadcasted_iota(jnp.int32, (chunk, rows), 0) + k * chunk
        ones = jnp.where(atom == index_row, F32(1), F32(0)).astype(BF16)
        part[pl.ds(k * chunk, chunk)] = jnp.dot(ones, values_ref[...], preferred_element_type=F32)

    def gather(full, column, k):
        values = full[pl.ds(k * chunk, chunk)]
        upper = values.astype(BF16)
        high[...] = upper
        low[...] = (values - upper.astype(F32)).astype(BF16)

        @pl.loop(0, rows // TILE)
        def _(t):
            tile = rows_at(t * TILE, TILE)
            index = column[tile]
            lane = lax.broadcasted_iota(jnp.int32, index.shape, 1) + k * chunk
            ones = jnp.concatenate(
                [
                    jnp.where(index == lane + 128 * j, F32(1), F32(0)).astype(BF16)
                    for j in range(chunk // 128)
                ],
                axis=1,
            )
            total = jnp.dot(ones, high[...], preferred_element_type=F32)
            total = total + jnp.dot(ones, low[...], preferred_element_type=F32)
            if k == 0:
                message[tile] = total
            else:
                message[tile] = message[tile] + total

    def layer(values_ref, column, inner_ref, outer_ref, gain_ref, result_ref):
        @pl.loop(0, rows // TILE)
        def _(t):
            tile = rows_at(t * TILE, TILE)
            m = message[tile] - values_ref[tile].astype(F32)
            mean_square = jnp.mean(m * m, axis=-1, keepdims=True)
            normed = m * lax.rsqrt(mean_square + 1e-5) * gain_ref[...]
            activated = jnp.dot(normed.astype(BF16), inner_ref[...], preferred_element_type=F32)
            activated = jnp.maximum(activated, F32(0)).astype(BF16)
            result = normed + jnp.dot(activated, outer_ref[...], preferred_element_type=F32)
            keep = column[tile][:, :1] >= 0
            result_ref[tile] = jnp.where(keep, result, F32(0)).astype(BF16)

    copies = Copies(send_sems, recv_sems)

    scatter(part_one, state_ref, target_row, 0)
    pl.semaphore_wait(barrier, len(partners))

    class LayerOne:
        def __init__(self, k):
            self.k = k
            half = chunk // RING // 2
            self.half = half
            self.ring = Ring(
                copies, y, y_after, y_before, k * chunk, half, relay_one.at[k], direct_one.at[k], second_one.at[k]
            )
            self.steps = [self.s0, self.s1, self.s2, self.s3, self.s4, self.s5, self.s6, self.s7]

        def s0(self):
            if self.k > 0:
                scatter(part_one, state_ref, target_row, self.k)
            self.ring.reduce_first(part_one)

        def s1(self):
            self.ring.reduce_second(part_one)

        def s2(self):
            low_half, high_half = self.ring.reduce_last(part_one)
            k, half = self.k, self.half
            shard_one[k, 0:half] = low_half
            shard_one[k, half : 2 * half] = high_half
            self.near = copies.start(
                shard_one.at[k, rows_at((1 - parity) * half, half)], cross_one.at[k, 0], z_near
            )

        def s3(self):
            k, half = self.k, self.half
            self.near.wait_recv()
            mine = rows_at(parity * half, half)
            shard_one[k, mine] = shard_one[k, mine] + cross_one[k, 0]
            self.far = copies.start(shard_one.at[k, mine], cross_one.at[k, 1], z_far)

        def s4(self):
            k, half = self.k, self.half
            self.far.wait_recv()
            mine = rows_at(k * chunk + y * (2 * half) + parity * half, half)
            full_one[mine] = shard_one[k, rows_at(parity * half, half)] + cross_one[k, 1]
            self.back = copies.start(full_one.at[mine], full_one.at[mine], z_near)

        def s5(self):
            self.back.wait_recv()
            self.ring.gather_first(full_one)

        def s6(self):
            self.ring.gather_second(full_one)

        def s7(self):
            self.ring.gather_last()
            gather(full_one, column_one, self.k)

    class LayerTwo:
        def __init__(self, k):
            self.k = k
            side = chunk // 2
            self.side = side
            self.base = k * chunk + core * side
            half = side // RING // 2
            self.half = half
            self.ring = Ring(
                copies, x, x_after, x_before, self.base, half, relay_two.at[k], direct_two.at[k], second_two.at[k]
            )
            self.steps = [self.s0, self.s1, self.s2, self.s3, self.s4, self.s5, self.s6, self.s7]

        def s0(self):
            k = self.k
            scatter(part_two, reverse, source_row, k)
            theirs = rows_at(k * chunk + (1 - core) * self.side, self.side)
            self.pair = copies.start(part_two.at[theirs], pair_two.at[k], sibling)

        def s1(self):
            self.pair.wait_recv()
            mine = rows_at(self.base, self.side)
            part_two[mine] = part_two[mine] + pair_two[self.k]
            self.ring.reduce_first(part_two)

        def s2(self):
            self.ring.reduce_second(part_two)

        def s3(self):
            low_half, high_half = self.ring.reduce_last(part_two)
            low_rows, high_rows = self.ring.at(0, 0), self.ring.at(0, 1)
            part_two[low_rows] = low_half
            part_two[high_rows] = high_half
            self.own = rows_at(self.base + x * (2 * self.half), 2 * self.half)
            self.across = copies.start(part_two.at[self.own], cross_two.at[self.k], z_across)

        def s4(self):
            self.across.wait_recv()
            full_two[self.own] = part_two[self.own] + cross_two[self.k]
            self.ring.gather_first(full_two)

        def s5(self):
            self.ring.gather_second(full_two)

        def s6(self):
            self.ring.gather_last()
            mine = rows_at(self.base, self.side)
            self.back = copies.start(full_two.at[mine], full_two.at[mine], sibling)

        def s7(self):
            self.back.wait_recv()
            gather(full_two, column_two, self.k)

    def run(parts):
        n = len(parts[0].steps)
        for t in range(n + CHUNKS - 1):
            for k in range(CHUNKS):
                if 0 <= t - k < n:
                    parts[k].steps[t - k]()
            if t == 0 and parts[0].__class__ is LayerOne:
                column_one[...] = jnp.transpose(jnp.broadcast_to(target_row, (128, rows)))
                column_two[...] = jnp.transpose(jnp.broadcast_to(source_row, (128, rows)))

    run([LayerOne(k) for k in range(CHUNKS)])
    layer(state_ref, column_one, inner_one_ref, outer_one_ref, gain_one_ref, reverse)
    run([LayerTwo(k) for k in range(CHUNKS)])
    layer(reverse, column_two, inner_two_ref, outer_two_ref, gain_two_ref, out_ref)

    for copy in copies.made:
        copy.wait_send()


COPIES_PER_CHUNK = 6 + 3 + 6 + 1 + 6 + 1 + 6 + 1


def body(
    edge_state,
    edge_source,
    edge_target,
    live_edges,
    inner_one,
    outer_one,
    inner_two,
    outer_two,
    gain_one,
    gain_two,
):
    rows, channels = edge_state.shape[2:]
    atoms = 1024
    chunk = atoms // CHUNKS
    half_one, half_two = chunk // RING // 2, chunk // 2 // RING // 2
    vmem = pl.BlockSpec(memory_space=pltpu.VMEM)
    smem = pl.BlockSpec(memory_space=pltpu.SMEM)

    def piece(*shape):
        return pltpu.VMEM((CHUNKS, *shape, channels), F32)

    result = pl.pallas_call(
        kernel,
        out_shape=jax.ShapeDtypeStruct((rows, channels), BF16),
        in_specs=[vmem, vmem, vmem, smem] + [vmem] * 6,
        out_specs=vmem,
        scratch_shapes=[
            pltpu.VMEM((atoms, channels), F32),
            pltpu.VMEM((atoms, channels), F32),
            pltpu.VMEM((atoms, channels), F32),
            pltpu.VMEM((atoms, channels), F32),
            pltpu.VMEM((rows, channels), F32),
            pltpu.VMEM((rows, channels), BF16),
            pltpu.VMEM((chunk, channels), BF16),
            pltpu.VMEM((chunk, channels), BF16),
            pltpu.VMEM((rows, 128), jnp.int32),
            pltpu.VMEM((rows, 128), jnp.int32),
            piece(2, half_one),
            piece(2, half_one),
            piece(2, half_one),
            piece(2 * half_one),
            piece(2, half_one),
            piece(2, half_two),
            piece(2, half_two),
            piece(2, half_two),
            piece(chunk // 2),
            piece(2 * half_two),
            pltpu.SemaphoreType.DMA((COPIES_PER_CHUNK * CHUNKS,)),
            pltpu.SemaphoreType.DMA((COPIES_PER_CHUNK * CHUNKS,)),
        ],
        compiler_params=pltpu.CompilerParams(
            collective_id=0, has_side_effects=True, vmem_limit_bytes=48 * 2**20
        ),
    )(
        edge_state.reshape(rows, channels),
        edge_source.reshape(1, rows),
        edge_target.reshape(1, rows),
        live_edges,
        inner_one,
        outer_one,
        inner_two,
        outer_two,
        gain_one.reshape(1, channels),
        gain_two.reshape(1, channels),
    )
    return result.reshape(1, 1, rows, channels)


def solution(mesh):
    placed = (
        P("src", "tgt", None, None),
        P("src", "tgt", None),
        P("src", "tgt", None),
        P("src", "tgt"),
        P(),
        P(),
        P(),
        P(),
        P(),
        P(),
    )
    return jax.shard_map(
        body, mesh=mesh, in_specs=placed, out_specs=P("src", "tgt", None, None), check_vma=False
    )
```

time: 435 us -> 113 us (0.26)
  waiting for transfers between devices: 362 us -> 0 us
  Pallas kernels: 0 us -> 104 us
  other arithmetic: 23 us -> 0 us
  local copies, waits for them, and re-layouts: 26.2 us -> 7.72 us
  between operations: 14.1 us -> 0.71 us
  matrix products: 10.1 us -> 0 us
    psum x2 -> x0, waiting for transfers between devices: 362 us -> none  [the longest x1 191 us: source_totals(): return lax.psum(partial_value, 'tgt')]
    pallas_call x0 -> x1, Pallas kernels: none -> 104 us  [body(): pl.pallas_call(kernel, out_shape=jax.ShapeDtypeStruct((rows, channels), B...]
    gather x4 -> x0, local copies, waits for them, and re-layouts: 17.3 us -> none  [the longest x2 9.84 us: body(): message = jnp.take(incoming, targets, axis=0) - states.astype(jnp.float32)]
    scatter-add x2 -> x0, other arithmetic: 16.6 us -> none  [the longest x1 8.63 us: body(): jax.ops.segment_sum(jnp.where(alive[:, None], states.astype(jnp.float32),...]
    dot_general x2 -> x0, matrix products: 10.1 us -> none  [update_edges(): jnp.dot(activated, outer, preferred_element_type=jnp.float32)]
    unnamed x17 -> x19, local copies, waits for them, and re-layouts: 1.76 us -> 7.72 us
    reduce_sum x2 -> x0, other arithmetic: 4.76 us -> none  [update_edges(): mean_square = jnp.mean(message * message, axis=-1, keepdims=True)]
  transfers between devices with their start and end apart: 2 -> 0, of which waited for: 2 -> 0; matrix products, arithmetic and copies ran while one was open for 0% -> 0% of each run, Pallas kernels for 0% -> 0%
where the time goes in v1:
time: 113 us
  Pallas kernels  104 us (92%)
  local copies, waits for them, and re-layouts  7.72 us (7%)
    pallas_call x1, Pallas kernels, body(): pl.pallas_call(kernel, out_shape=jax.ShapeDtypeStruct((rows, channels), B...  104 us
    unnamed x19, local copies, waits for them, and re-layouts  7.72 us

profile of v1, /device:TPU:1, one launch (start us, length us, event | category | flops | bytes accessed | tf_op | source)
XLA Modules:
  0.0 112.7 jit_solution(12150470982034387258)
XLA Ops:
  0.0 0.0 copy-start.7
  0.7 0.0 copy-start.6
  0.7 0.0 copy-start.5
  0.7 0.0 copy-done.7
  0.7 0.7 copy-done.6
  1.4 0.0 copy-done.5
  1.4 0.0 copy-start
  1.4 1.2 %copy-done = bf16[1,1,1024,512]{3,2,1,0:T(8,128)(2,1)S(1)} copy-done((bf16[1,1,1024,512]{3,2,1,0:T(8,128)(2,1)S(1)}, bf16[1,1,1024,512]{3,2,1,0:T(8,128)(2,1)}, u32[]{:S(2)}) %copy-start) | copy-done | bytes 1048600
  2.6 0.0 copy-start.1
  2.6 1.0 copy-done.1
  3.6 0.0 copy-start.2
  3.6 1.0 copy-done.2
  4.7 0.0 copy-start.3
  4.7 1.0 copy-done.3
  5.7 0.0 copy-start.4
  5.7 1.0 copy-done.4
  6.8 0.0 copy-start.8
  6.8 0.7 copy-done.8
  7.4 104.2 %shard_map.100 = bf16[1024,512]{1,0:T(8,128)(2,1)S(1)} custom-call(bf16[1024,512]{1,0:T(8,128)(2,1)S(1)} %bitcast.7, s32[1,1024]{1,0:T(1,128)S(1)} %bitcast.8, s32[1,1024]{1,0:T(1,128)S(1)} %bitcast.9, s32[1,1]{1,0:T(1,128)S(6)} %copy.12.live_ref, bf16[512,512]{1,0:T(8,128)(2,1)S(1)} %copy-done.1, bf16[512,512]{1,0:T(8,128)(2,1)S(1)} %copy-done.2, ...), custom_call_target="tpu_custom_call" | custom-call | tf_op jit(solution)/shard_map/pallas_call | solution.py:360
  111.7 1.0 copy.13
Async XLA Ops:
  0.0 0.7 copy-start.7
  0.7 0.7 copy-start.6
  0.7 0.7 copy-start.5
  1.4 1.2 %copy-start = (bf16[1,1,1024,512]{3,2,1,0:T(8,128)(2,1)S(1)}, bf16[1,1,1024,512]{3,2,1,0:T(8,128)(2,1)}, u32[]{:S(2)}) copy-start(bf16[1,1,1024,512]{3,2,1,0:T(8,128)(2,1)} %param.10) | copy-start | bytes 3145732
  2.6 1.0 copy-start.1
  3.6 1.0 copy-start.2
  4.7 1.0 copy-start.3
  5.7 1.0 copy-start.4
  6.8 0.7 copy-start.8

commit v2 on v0

v2 whole, which is shorter than its diff:
```python
import functools

import jax
import jax.numpy as jnp
from jax import lax
from jax.experimental import pallas as pl
from jax.experimental.pallas import tpu as pltpu
from jax.sharding import PartitionSpec as P

MESH = pl.DeviceIdType.MESH
RING = 4
TILE = 512
BLOCK = 256
LANES = 128
BF16 = jnp.bfloat16
F32 = jnp.float32

KINDS_ONE = ('AA', 'AB', 'AB', 'AA', 'BB', 'BA', 'AA', 'BB')
ORDER_ONE = (4, 0, 2, 5, 1, 0, 7, 3, 1, 2, 6, 0, 3, 4, 1, 5, 2, 6, 0, 3, 4, 1, 7, 5, 2, 6, 4, 3, 0, 5, 7, 1, 2, 6, 7, 1, 0, 4, 3, 2, 1, 5, 6, 0, 1, 4, 4, 7, 2, 3, 5, 2, 1, 7, 6, 4, 0, 7, 5, 3, 7, 6, 2, 4, 5, 3, 7, 6)
ORDER_TWO = (0, 6, 1, 2, 0, 3, 4, 1, 2, 5, 0, 3, 1, 2, 4, 0, 3, 5, 1, 6, 7, 4, 2, 7, 5, 3, 4, 6, 7, 5, 1, 0, 6, 2, 7, 3, 1, 4, 0, 2, 5, 6, 4, 7, 0, 1, 5, 3, 4, 6, 2, 1, 7, 0, 5, 3, 2, 4, 6, 7, 3, 5, 6, 7)
PLACE_ONE = (1, 0, 2, 5, 3, 4, 7, 6)
PLACE_TWO = (1, 0, 2, 4, 3, 5, 6, 7)


class Copies:
    def __init__(self, inbox, send_sem, recv_sems):
        self.inbox, self.send_sem, self.recv_sems = inbox, send_sem, recv_sems
        self.groups = self.used = self.sent = 0

    def group(self):
        self.groups += 1
        return self.groups - 1

    def room(self, count):
        room = pl.ds(self.used, count)
        self.used += count
        return room

    def start(self, src, dst, device, group):
        self.sent += src.shape[0]
        pltpu.make_async_remote_copy(
            src_ref=src,
            dst_ref=dst,
            send_sem=self.send_sem,
            recv_sem=self.recv_sems.at[group],
            device_id=device,
            device_id_type=MESH,
        ).start()

    def push(self, ref, rows, device, group):
        self.start(ref.at[rows], ref.at[rows], device, group)

    def hand(self, ref, rows, count, device, group):
        room = self.room(count)
        self.start(ref.at[rows], self.inbox.at[room], device, group)
        return room

    def wait(self, sem, count):
        rows = self.inbox.at[pl.ds(0, count)]
        pltpu.make_async_copy(rows, rows, sem).wait()

    def arrived(self, group, count):
        self.wait(self.recv_sems.at[group], count)

    def all_sent(self):
        self.wait(self.send_sem, self.sent)


def rows_at(offset, count):
    return pl.ds(pl.multiple_of(offset, 8), count)


class Ring:
    def __init__(self, copies, me, after, before, base, shard_stride, part_stride, count):
        self.copies, self.me, self.after, self.before = copies, me, after, before
        self.base, self.shard_stride, self.part_stride, self.count = base, shard_stride, part_stride, count

    def at(self, step, part):
        shard = (self.me + step + RING) % RING
        return rows_at(self.base + shard * self.shard_stride + part * self.part_stride, self.count)

    def reduce_first(self, data):
        self.relay_group, self.reduce_group = self.copies.group(), self.copies.group()

        def hand(step, part, device, group):
            return self.copies.hand(data, self.at(step, part), self.count, device, group)

        self.relays = [hand(2, 0, self.after, self.relay_group), hand(2, 1, self.before, self.relay_group)]
        self.directs = [hand(1, 1, self.after, self.reduce_group), hand(-1, 0, self.before, self.reduce_group)]

    def reduce_second(self, data):
        self.copies.arrived(self.relay_group, 2 * self.count)
        self.seconds = []
        for way, (step, device) in enumerate(((1, self.after), (-1, self.before))):
            rows = self.at(step, way)
            data[rows] = data[rows] + self.copies.inbox[self.relays[way]]
            self.seconds.append(self.copies.hand(data, rows, self.count, device, self.reduce_group))

    def reduce_last(self, data):
        self.copies.arrived(self.reduce_group, 4 * self.count)
        inbox = self.copies.inbox
        for way in range(2):
            rows = self.at(0, way)
            data[rows] = data[rows] + inbox[self.directs[1 - way]] + inbox[self.seconds[way]]

    def gather_first(self, full):
        low, high = self.at(0, 0), self.at(0, 1)
        self.first_group, self.near_group, self.last_group = [self.copies.group() for _ in range(3)]
        push = self.copies.push
        push(full, low, self.after, self.first_group)
        push(full, high, self.before, self.first_group)
        push(full, high, self.after, self.near_group)
        push(full, low, self.before, self.near_group)

    def gather_second(self, full):
        self.copies.arrived(self.first_group, 2 * self.count)
        self.copies.push(full, self.at(-1, 0), self.after, self.last_group)
        self.copies.push(full, self.at(1, 1), self.before, self.last_group)

    def gather_near(self):
        self.copies.arrived(self.near_group, 2 * self.count)

    def gather_last(self):
        self.copies.arrived(self.last_group, 2 * self.count)


def kernel(
    state_hbm,
    source_hbm,
    target_hbm,
    live_hbm,
    inner_one_hbm,
    outer_one_hbm,
    inner_two_hbm,
    outer_two_hbm,
    gain_one_hbm,
    gain_two_hbm,
    out_ref,
    state_ref,
    source_ref,
    target_ref,
    live_ref,
    inner_one_ref,
    outer_one_ref,
    inner_two_ref,
    outer_two_ref,
    gain_one_ref,
    gain_two_ref,
    part_one,
    part_two,
    full_one,
    full_two,
    message,
    reverse,
    high,
    low,
    ones_one,
    ones_two,
    inbox,
    local_sems,
    send_sems,
    recv_sems,
):
    rows, channels = state_ref.shape
    atoms = part_one.shape[0]

    src, tgt = lax.axis_index("src"), lax.axis_index("tgt")
    y, z_lo = src // 4, src % 4
    z_hi, x, core = tgt // 8, (tgt // 2) % 4, tgt % 2
    y_after, y_before = (((y + 1) % 4) * 4 + z_lo, tgt), (((y + 3) % 4) * 4 + z_lo, tgt)
    parity = z_lo % 2
    z_near, z_far = (y * 4 + z_lo + 1 - 2 * parity, tgt), (y * 4 + (z_lo + 2) % 4, tgt)
    sibling = (src, tgt + 1 - 2 * core)
    x_after = (src, z_hi * 8 + ((x + 1) % 4) * 2 + core)
    x_before = (src, z_hi * 8 + ((x + 3) % 4) * 2 + core)
    z_across = (src, (1 - z_hi) * 8 + x * 2 + core)

    barrier = pltpu.get_barrier_semaphore()
    partners = (y_after, y_before, z_near, z_far, sibling, x_after, x_before, z_across)
    for device in partners:
        pl.semaphore_signal(barrier, inc=1, device_id=device, device_id_type=MESH)

    loads = []
    for i, (far, near) in enumerate(
        (
            (live_hbm, live_ref),
            (target_hbm, target_ref),
            (state_hbm, state_ref),
            (source_hbm, source_ref),
            (inner_one_hbm, inner_one_ref),
            (outer_one_hbm, outer_one_ref),
            (gain_one_hbm, gain_one_ref),
            (inner_two_hbm, inner_two_ref),
            (outer_two_hbm, outer_two_ref),
            (gain_two_hbm, gain_two_ref),
        )
    ):
        load = pltpu.make_async_copy(far, near, local_sems.at[i])
        load.start()
        loads.append(load)
    for load in loads[:3]:
        load.wait()

    live = live_ref[0, 0]
    alive = lax.broadcasted_iota(jnp.int32, (1, rows), 1) < live

    def index_of(index_ref):
        return jnp.where(alive, index_ref[...], -1)

    def scatter(part, values_ref, index_ref, block):
        atom = lax.broadcasted_iota(jnp.int32, (BLOCK, rows), 0) + block * BLOCK
        ones = jnp.where(atom == index_of(index_ref), F32(1), F32(0)).astype(BF16)
        part[pl.ds(block * BLOCK, BLOCK)] = jnp.dot(ones, values_ref[...], preferred_element_type=F32)

    def mark(ones_ref, index_ref):
        for t in range(rows // LANES):
            row = jnp.where(
                lax.broadcasted_iota(jnp.int32, (1, LANES), 1) + t * LANES < live,
                index_ref[:, pl.ds(t * LANES, LANES)],
                -1,
            )
            column = jnp.transpose(jnp.broadcast_to(row, (LANES, LANES)))
            lane = lax.broadcasted_iota(jnp.int32, (LANES, LANES), 1)
            for j in range(atoms // LANES):
                ones_ref[pl.ds(t * LANES, LANES), pl.ds(j * LANES, LANES)] = jnp.where(
                    column == lane + j * LANES, F32(1), F32(0)
                ).astype(BF16)

    def gather(full, ones_ref, block, values_ref, first):
        values = full[pl.ds(block * BLOCK, BLOCK)]
        upper = values.astype(BF16)
        high[...] = upper
        low[...] = (values - upper.astype(F32)).astype(BF16)

        for t in range(rows // TILE):
            tile = pl.ds(t * TILE, TILE)
            ones = ones_ref[tile, pl.ds(block * BLOCK, BLOCK)]
            total = jnp.dot(ones, high[...], preferred_element_type=F32)
            total = total + jnp.dot(ones, low[...], preferred_element_type=F32)
            if first:
                message[tile] = total - values_ref[tile].astype(F32)
            else:
                message[tile] = message[tile] + total

    def layer(inner_ref, outer_ref, gain_ref, result_ref):
        for t in range(rows // TILE):
            tile = pl.ds(t * TILE, TILE)
            m = message[tile]
            mean_square = jnp.mean(m * m, axis=-1, keepdims=True)
            normed = m * lax.rsqrt(mean_square + 1e-5) * gain_ref[...]
            activated = jnp.dot(normed.astype(BF16), inner_ref[...], preferred_element_type=F32)
            activated = jnp.maximum(activated, F32(0)).astype(BF16)
            result = normed + jnp.dot(activated, outer_ref[...], preferred_element_type=F32)
            keep = lax.broadcasted_iota(jnp.int32, (TILE, channels), 0) + t * TILE < live
            result_ref[tile] = jnp.where(keep, result, F32(0)).astype(BF16)

    copies = Copies(inbox, send_sems.at[0], recv_sems)

    class LayerOne:
        def __init__(self, kind, base, size):
            self.size = size
            reduce_kind, gather_kind = kind
            eighth = size // 8
            if reduce_kind == "A":
                shard_stride, part_stride = 2 * eighth, eighth
                self.reduce_ring = self.ring(base, shard_stride, part_stride, eighth)
                self.mine = rows_at(base + y * shard_stride + parity * part_stride, eighth)
                self.theirs = rows_at(base + y * shard_stride + (1 - parity) * part_stride, eighth)
                steps = [self.ring_first, self.ring_second, self.ring_then_near, self.near_then_far]
            else:
                shard_stride, part_stride = eighth, 4 * eighth
                self.reduce_ring = self.ring(base + parity * part_stride, shard_stride, eighth // 2, eighth // 2)
                self.mine = rows_at(base + y * shard_stride + parity * part_stride, eighth)
                self.upper = rows_at(base + parity * part_stride, part_stride)
                self.lower = rows_at(base + (1 - parity) * part_stride, part_stride)
                steps = [self.near_first, self.near_then_ring, self.ring_second, self.ring_then_far]
            if gather_kind == "A":
                self.gather_ring = self.ring(base, shard_stride, part_stride, eighth)
                steps += [self.far_then_near, self.near_then_gather, self.gather_second, self.gather_end]
            else:
                self.gather_ring = self.ring(
                    base + parity * part_stride, shard_stride, eighth // 2, eighth // 2
                )
                steps += [self.far_then_gather, self.gather_second, self.near_backs, self.last_backs, self.backs_end]
            self.steps = steps

            def shard(step):
                return rows_at(base + ((y + step) % RING) * shard_stride + parity * part_stride, eighth)

            self.shard = shard

        def ring(self, *where):
            return Ring(copies, y, y_after, y_before, *where)

        def ring_first(self):
            self.reduce_ring.reduce_first(part_one)

        def ring_second(self):
            self.reduce_ring.reduce_second(part_one)

        def hand(self, rows, count, device):
            group = copies.group()
            return group, copies.hand(part_one, rows, count, device, group), count

        def add(self, rows, handed, result):
            group, room, count = handed
            copies.arrived(group, count)
            result[rows] = part_one[rows] + inbox[room]

        def ring_then_near(self):
            self.reduce_ring.reduce_last(part_one)
            self.near = self.hand(self.theirs, self.size // 8, z_near)

        def near_then_far(self):
            self.add(self.mine, self.near, part_one)
            self.far = self.hand(self.mine, self.size // 8, z_far)

        def near_first(self):
            self.near = self.hand(self.lower, self.size // 2, z_near)

        def near_then_ring(self):
            self.add(self.upper, self.near, part_one)
            self.reduce_ring.reduce_first(part_one)

        def ring_then_far(self):
            self.reduce_ring.reduce_last(part_one)
            self.far = self.hand(self.mine, self.size // 8, z_far)

        def far_then_near(self):
            self.add(self.mine, self.far, full_one)
            self.back = copies.group()
            copies.push(full_one, self.mine, z_near, self.back)

        def near_then_gather(self):
            copies.arrived(self.back, self.size // 8)
            self.gather_ring.gather_first(full_one)

        def gather_second(self):
            self.gather_ring.gather_second(full_one)

        def gather_end(self):
            self.gather_ring.gather_near()
            self.gather_ring.gather_last()

        def far_then_gather(self):
            self.add(self.mine, self.far, full_one)
            self.gather_ring.gather_first(full_one)
            self.back = copies.group()
            copies.push(full_one, self.mine, z_near, self.back)

        def near_backs(self):
            self.gather_ring.gather_near()
            for step in (1, 3):
                copies.push(full_one, self.shard(step), z_near, self.back)

        def last_backs(self):
            self.gather_ring.gather_last()
            copies.push(full_one, self.shard(2), z_near, self.back)

        def backs_end(self):
            copies.arrived(self.back, self.size // 2)

    class LayerTwo:
        def __init__(self, base, size):
            side = size // 2
            self.side, self.eighth = side, side // 8
            self.ours, self.theirs = rows_at(base + core * side, side), rows_at(base + (1 - core) * side, side)
            self.own = rows_at(base + core * side + x * (2 * self.eighth), 2 * self.eighth)
            self.ring = Ring(
                copies, x, x_after, x_before, base + core * side, 2 * self.eighth, self.eighth, self.eighth
            )
            self.steps = [
                self.pair_first,
                self.pair_then_ring,
                self.ring_second,
                self.ring_then_across,
                self.across_then_gather,
                self.gather_second,
                self.gather_then_pair,
                self.pair_end,
            ]

        def pair_first(self):
            self.pair = copies.group()
            self.pair_room = copies.hand(part_two, self.theirs, self.side, sibling, self.pair)

        def pair_then_ring(self):
            copies.arrived(self.pair, self.side)
            part_two[self.ours] = part_two[self.ours] + inbox[self.pair_room]
            self.ring.reduce_first(part_two)

        def ring_second(self):
            self.ring.reduce_second(part_two)

        def ring_then_across(self):
            self.ring.reduce_last(part_two)
            self.across = copies.group()
            self.across_room = copies.hand(part_two, self.own, 2 * self.eighth, z_across, self.across)

        def across_then_gather(self):
            copies.arrived(self.across, 2 * self.eighth)
            full_two[self.own] = part_two[self.own] + inbox[self.across_room]
            self.ring.gather_first(full_two)

        def gather_second(self):
            self.ring.gather_second(full_two)

        def gather_then_pair(self):
            self.ring.gather_near()
            self.ring.gather_last()
            self.back = copies.group()
            copies.push(full_two, self.ours, sibling, self.back)

        def pair_end(self):
            copies.arrived(self.back, self.side)

    def run(chunks, order, places, scatter_block, gather_block, aside=None):
        per_block = BLOCK // (atoms // len(chunks))
        done = [0] * len(chunks)
        scattered, ended, gathered = set(), {}, 0
        for i, k in enumerate(order):
            if i == len(chunks) and aside is not None:
                aside()
            block = places[k] // per_block
            if block not in scattered:
                scattered.add(block)
                scatter_block(block)
            chunks[k].steps[done[k]]()
            done[k] += 1
            if done[k] == len(chunks[k].steps):
                ended[block] = ended.get(block, 0) + 1
                if ended[block] == per_block:
                    gather_block(block, gathered == 0)
                    gathered += 1
        assert all(d == len(c.steps) for d, c in zip(done, chunks))

    def scatter_one(block):
        scatter(part_one, state_ref, target_ref, block)
        if block == PLACE_ONE[ORDER_ONE[0]] // (BLOCK * len(KINDS_ONE) // atoms):
            pl.semaphore_wait(barrier, len(partners))

    size_one = atoms // len(KINDS_ONE)
    chunks_one = [LayerOne(kind, place * size_one, size_one) for kind, place in zip(KINDS_ONE, PLACE_ONE)]
    size_two = atoms // len(PLACE_TWO)
    chunks_two = [LayerTwo(place * size_two, size_two) for place in PLACE_TWO]

    def mark_both():
        for load in loads[3:]:
            load.wait()
        mark(ones_one, target_ref)
        mark(ones_two, source_ref)

    def gather_one(block, first):
        gather(full_one, ones_one, block, state_ref, first)

    run(chunks_one, ORDER_ONE, PLACE_ONE, scatter_one, gather_one, mark_both)
    copies.all_sent()
    copies.send_sem, copies.sent = send_sems.at[1], 0
    layer(inner_one_ref, outer_one_ref, gain_one_ref, reverse)

    def gather_two(block, first):
        gather(full_two, ones_two, block, reverse, first)

    run(
        chunks_two,
        ORDER_TWO,
        PLACE_TWO,
        lambda block: scatter(part_two, reverse, source_ref, block),
        gather_two,
    )
    layer(inner_two_ref, outer_two_ref, gain_two_ref, out_ref)

    copies.all_sent()
    assert copies.groups == GROUPS


GROUPS = 8 * (len(KINDS_ONE) + len(PLACE_TWO))


def body(
    edge_state,
    edge_source,
    edge_target,
    live_edges,
    inner_one,
    outer_one,
    inner_two,
    outer_two,
    gain_one,
    gain_two,
):
    rows, channels = edge_state.shape[2:]
    atoms = 1024
    operands = (
        edge_state.reshape(rows, channels),
        edge_source.reshape(1, rows),
        edge_target.reshape(1, rows),
        live_edges,
        inner_one,
        outer_one,
        inner_two,
        outer_two,
        gain_one.reshape(1, channels),
        gain_two.reshape(1, channels),
    )

    def copy_of(i, operand):
        space = pltpu.SMEM if i == 3 else pltpu.VMEM
        return space(operand.shape, operand.dtype)

    result = pl.pallas_call(
        kernel,
        out_shape=jax.ShapeDtypeStruct((rows, channels), BF16),
        in_specs=[pl.BlockSpec(memory_space=pltpu.HBM)] * len(operands),
        out_specs=pl.BlockSpec(memory_space=pltpu.VMEM),
        scratch_shapes=[copy_of(i, operand) for i, operand in enumerate(operands)]
        + [
            pltpu.VMEM((atoms, channels), F32),
            pltpu.VMEM((atoms, channels), F32),
            pltpu.VMEM((atoms, channels), F32),
            pltpu.VMEM((atoms, channels), F32),
            pltpu.VMEM((rows, channels), F32),
            pltpu.VMEM((rows, channels), BF16),
            pltpu.VMEM((BLOCK, channels), BF16),
            pltpu.VMEM((BLOCK, channels), BF16),
            pltpu.VMEM((rows, atoms), BF16),
            pltpu.VMEM((rows, atoms), BF16),
            pltpu.VMEM((2 * atoms, channels), F32),
            pltpu.SemaphoreType.DMA((len(operands),)),
            pltpu.SemaphoreType.DMA((2,)),
            pltpu.SemaphoreType.DMA((GROUPS,)),
        ],
        compiler_params=pltpu.CompilerParams(
            collective_id=0, has_side_effects=True, vmem_limit_bytes=56 * 2**20
        ),
    )(*operands)
    return result.reshape(1, 1, rows, channels)


def solution(mesh):
    placed = (
        P("src", "tgt", None, None),
        P("src", "tgt", None),
        P("src", "tgt", None),
        P("src", "tgt"),
        P(),
        P(),
        P(),
        P(),
        P(),
        P(),
    )
    return jax.shard_map(
        body, mesh=mesh, in_specs=placed, out_specs=P("src", "tgt", None, None), check_vma=False
    )
```

time: 435 us -> 89.2 us (0.21)
  waiting for transfers between devices: 362 us -> 0 us
  Pallas kernels: 0 us -> 86.2 us
  local copies, waits for them, and re-layouts: 26.2 us -> 2.26 us
  other arithmetic: 23 us -> 0 us
  between operations: 14.1 us -> 0.66 us
  matrix products: 10.1 us -> 0 us
    psum x2 -> x0, waiting for transfers between devices: 362 us -> none  [the longest x1 191 us: source_totals(): return lax.psum(partial_value, 'tgt')]
    pallas_call x0 -> x1, Pallas kernels: none -> 86.2 us  [body(): pl.pallas_call(kernel, out_shape=jax.ShapeDtypeStruct((rows, channels), B...]
    gather x4 -> x0, local copies, waits for them, and re-layouts: 17.3 us -> none  [the longest x2 9.84 us: body(): message = jnp.take(incoming, targets, axis=0) - states.astype(jnp.float32)]
    scatter-add x2 -> x0, other arithmetic: 16.6 us -> none  [the longest x1 8.63 us: body(): jax.ops.segment_sum(jnp.where(alive[:, None], states.astype(jnp.float32),...]
    dot_general x2 -> x0, matrix products: 10.1 us -> none  [update_edges(): jnp.dot(activated, outer, preferred_element_type=jnp.float32)]
    reduce_sum x2 -> x0, other arithmetic: 4.76 us -> none  [update_edges(): mean_square = jnp.mean(message * message, axis=-1, keepdims=True)]
  transfers between devices with their start and end apart: 2 -> 0, of which waited for: 2 -> 0; matrix products, arithmetic and copies ran while one was open for 0% -> 0% of each run, Pallas kernels for 0% -> 0%
where the time goes in v2:
time: 89.2 us; the launch traced here: 89.1 us
  Pallas kernels  86.2 us (97%)
  local copies, waits for them, and re-layouts  2.26 us (3%)
    pallas_call x1, Pallas kernels, body(): pl.pallas_call(kernel, out_shape=jax.ShapeDtypeStruct((rows, channels), B...  86.2 us
    unnamed x1, local copies, waits for them, and re-layouts  2.26 us

profile of v2, /device:TPU:1, one launch (start us, length us, event | category | flops | bytes accessed | tf_op | source)
XLA Modules:
  0.0 89.1 jit_solution(7616175129477805138)
XLA Ops:
  0.7 86.2 %shard_map.100 = bf16[1024,512]{1,0:T(8,128)(2,1)} custom-call(bf16[1024,512]{1,0:T(8,128)(2,1)} %bitcast.7, s32[1,1024]{1,0:T(1,128)} %bitcast.8, s32[1,1024]{1,0:T(1,128)} %bitcast.9, s32[1,1]{1,0:T(1,128)S(6)} %copy.12.live_hbm, bf16[512,512]{1,0:T(8,128)(2,1)} %inner_one_hbm.1, bf16[512,512]{1,0:T(8,128)(2,1)} %outer_one_hbm.1, ...), custom_call_target="tpu_custom_call" | custom-call | tf_op jit(solution)/shard_map/pallas_call | solution.py:511
  86.8 2.3 %copy.13 = bf16[1,1,1024,512]{3,2,1,0:T(8,128)(2,1)} copy(bf16[1,1,1024,512]{3,2,1,0:T(8,128)(2,1)} %bitcast.6) | data formatting | bytes 2097152

commit v3 on v2

--- a/solution.py
+++ b/solution.py
@@ -10,16 +10,18 @@
 MESH = pl.DeviceIdType.MESH
 RING = 4
 TILE = 512
+CHUNK = 128
 BLOCK = 256
 LANES = 128
 BF16 = jnp.bfloat16
 F32 = jnp.float32
 
-KINDS_ONE = ('AA', 'AB', 'AB', 'AA', 'BB', 'BA', 'AA', 'BB')
-ORDER_ONE = (4, 0, 2, 5, 1, 0, 7, 3, 1, 2, 6, 0, 3, 4, 1, 5, 2, 6, 0, 3, 4, 1, 7, 5, 2, 6, 4, 3, 0, 5, 7, 1, 2, 6, 7, 1, 0, 4, 3, 2, 1, 5, 6, 0, 1, 4, 4, 7, 2, 3, 5, 2, 1, 7, 6, 4, 0, 7, 5, 3, 7, 6, 2, 4, 5, 3, 7, 6)
-ORDER_TWO = (0, 6, 1, 2, 0, 3, 4, 1, 2, 5, 0, 3, 1, 2, 4, 0, 3, 5, 1, 6, 7, 4, 2, 7, 5, 3, 4, 6, 7, 5, 1, 0, 6, 2, 7, 3, 1, 4, 0, 2, 5, 6, 4, 7, 0, 1, 5, 3, 4, 6, 2, 1, 7, 0, 5, 3, 2, 4, 6, 7, 3, 5, 6, 7)
-PLACE_ONE = (1, 0, 2, 5, 3, 4, 7, 6)
-PLACE_TWO = (1, 0, 2, 4, 3, 5, 6, 7)
+KINDS_ONE = ('BA', 'AA', 'AA', 'BB', 'AB', 'AA', 'BA', 'AB')
+KINDS_TWO = ('aA', 'aa', 'aa', 'aA', 'aa', 'aa', 'aa', 'aa')
+ORDER_ONE = (6, 5, 7, 0, 5, 4, 7, 6, 5, 2, 3, 4, 6, 7, 0, 2, 5, 1, 4, 6, 0, 3, 7, 1, 2, 4, 5, 0, 3, 1, 6, 2, 7, 3, 5, 4, 1, 6, 7, 0, 2, 7, 5, 4, 3, 6, 1, 0, 7, 4, 3, 2, 4, 5, 1, 3, 0, 3, 2, 6, 7, 1, 4, 0, 3, 2, 1)
+ORDER_TWO = (3, 1, 0, 6, 3, 7, 6, 1, 2, 5, 0, 2, 3, 4, 6, 5, 4, 1, 0, 7, 2, 3, 5, 6, 4, 1, 7, 3, 0, 2, 5, 1, 0, 4, 1, 6, 7, 2, 5, 6, 3, 2, 5, 4, 3, 0, 7, 4, 0, 7)
+PLACE_ONE = (4, 7, 6, 5, 3, 0, 1, 2)
+PLACE_TWO = (6, 0, 2, 4, 5, 3, 1, 7)
 
 
 class Copies:
@@ -71,8 +73,8 @@
 
 
 class Ring:
-    def __init__(self, copies, me, after, before, base, shard_stride, part_stride, count):
-        self.copies, self.me, self.after, self.before = copies, me, after, before
+    def __init__(self, copies, me, after, before, across, base, shard_stride, part_stride, count):
+        self.copies, self.me, self.after, self.before, self.across = copies, me, after, before, across
         self.base, self.shard_stride, self.part_stride, self.count = base, shard_stride, part_stride, count
 
     def at(self, step, part):
@@ -103,9 +105,10 @@
             rows = self.at(0, way)
             data[rows] = data[rows] + inbox[self.directs[1 - way]] + inbox[self.seconds[way]]
 
-    def gather_first(self, full):
+    def gather_first(self, full, apart=False):
         low, high = self.at(0, 0), self.at(0, 1)
-        self.first_group, self.near_group, self.last_group = [self.copies.group() for _ in range(3)]
+        self.first_group, self.near_group = self.copies.group(), self.copies.group()
+        self.last_group = self.copies.group() if apart else self.near_group
         push = self.copies.push
         push(full, low, self.after, self.first_group)
         push(full, high, self.before, self.first_group)
@@ -122,6 +125,32 @@
 
     def gather_last(self):
         self.copies.arrived(self.last_group, 2 * self.count)
+
+    def gather_rest(self):
+        self.copies.arrived(self.near_group, 4 * self.count)
+
+    def shard(self, step):
+        return rows_at(self.base + (self.me + step + RING) % RING * self.shard_stride, 2 * self.count)
+
+    def reduce_at_once(self, data):
+        self.reduce_group = self.copies.group()
+        self.terms = [
+            self.copies.hand(data, self.shard(step), 2 * self.count, device, self.reduce_group)
+            for step, device in ((1, self.after), (-1, self.before), (2, self.across))
+        ]
+
+    def reduce_at_once_last(self, data):
+        self.copies.arrived(self.reduce_group, 6 * self.count)
+        rows, inbox = self.shard(0), self.copies.inbox
+        data[rows] = data[rows] + inbox[self.terms[0]] + inbox[self.terms[1]] + inbox[self.terms[2]]
+
+    def gather_at_once(self, full):
+        self.near_group = self.copies.group()
+        for device in (self.after, self.before, self.across):
+            self.copies.push(full, self.shard(0), device, self.near_group)
+
+    def gather_at_once_last(self):
+        self.copies.arrived(self.near_group, 6 * self.count)
 
 
 def kernel(
@@ -152,8 +181,7 @@
     full_two,
     message,
     reverse,
-    high,
-    low,
+    terms,
     ones_one,
     ones_two,
     inbox,
@@ -173,10 +201,11 @@
     sibling = (src, tgt + 1 - 2 * core)
     x_after = (src, z_hi * 8 + ((x + 1) % 4) * 2 + core)
     x_before = (src, z_hi * 8 + ((x + 3) % 4) * 2 + core)
+    x_across = (src, z_hi * 8 + ((x + 2) % 4) * 2 + core)
     z_across = (src, (1 - z_hi) * 8 + x * 2 + core)
 
     barrier = pltpu.get_barrier_semaphore()
-    partners = (y_after, y_before, z_near, z_far, sibling, x_after, x_before, z_across)
+    partners = (y_after, y_before, z_near, z_far, sibling, x_after, x_before, x_across, z_across)
     for device in partners:
         pl.semaphore_signal(barrier, inc=1, device_id=device, device_id_type=MESH)
 
@@ -226,26 +255,31 @@
                     column == lane + j * LANES, F32(1), F32(0)
                 ).astype(BF16)
 
-    def gather(full, ones_ref, block, values_ref, first):
-        values = full[pl.ds(block * BLOCK, BLOCK)]
+    def pick(full, ones_ref, place, t):
+        ones = ones_ref[pl.ds(t * TILE, TILE), pl.ds(place * CHUNK, CHUNK)]
+        return jnp.dot(jnp.concatenate([ones, ones], axis=1), terms[...], preferred_element_type=F32)
+
+    def split(full, place):
+        values = full[pl.ds(place * CHUNK, CHUNK)]
         upper = values.astype(BF16)
-        high[...] = upper
-        low[...] = (values - upper.astype(F32)).astype(BF16)
-
+        terms[pl.ds(0, CHUNK)] = upper
+        terms[pl.ds(CHUNK, CHUNK)] = (values - upper.astype(F32)).astype(BF16)
+
+    def gather(full, ones_ref, place, values_ref, first):
+        split(full, place)
         for t in range(rows // TILE):
             tile = pl.ds(t * TILE, TILE)
-            ones = ones_ref[tile, pl.ds(block * BLOCK, BLOCK)]
-            total = jnp.dot(ones, high[...], preferred_element_type=F32)
-            total = total + jnp.dot(ones, low[...], preferred_element_type=F32)
+            total = pick(full, ones_ref, place, t)
             if first:
                 message[tile] = total - values_ref[tile].astype(F32)
             else:
                 message[tile] = message[tile] + total
 
-    def layer(inner_ref, outer_ref, gain_ref, result_ref):
+    def layer(full, ones_ref, place, inner_ref, outer_ref, gain_ref, result_ref):
+        split(full, place)
         for t in range(rows // TILE):
             tile = pl.ds(t * TILE, TILE)
-            m = message[tile]
+            m = message[tile] + pick(full, ones_ref, place, t)
             mean_square = jnp.mean(m * m, axis=-1, keepdims=True)
             normed = m * lax.rsqrt(mean_square + 1e-5) * gain_ref[...]
             activated = jnp.dot(normed.astype(BF16), inner_ref[...], preferred_element_type=F32)
@@ -290,7 +324,7 @@
             self.shard = shard
 
         def ring(self, *where):
-            return Ring(copies, y, y_after, y_before, *where)
+            return Ring(copies, y, y_after, y_before, None, *where)
 
         def ring_first(self):
             self.reduce_ring.reduce_first(part_one)
@@ -339,12 +373,11 @@
             self.gather_ring.gather_second(full_one)
 
         def gather_end(self):
-            self.gather_ring.gather_near()
-            self.gather_ring.gather_last()
+            self.gather_ring.gather_rest()
 
         def far_then_gather(self):
             self.add(self.mine, self.far, full_one)
-            self.gather_ring.gather_first(full_one)
+            self.gather_ring.gather_first(full_one, apart=True)
             self.back = copies.group()
             copies.push(full_one, self.mine, z_near, self.back)
 
@@ -361,24 +394,28 @@
             copies.arrived(self.back, self.size // 2)
 
     class LayerTwo:
-        def __init__(self, base, size):
+        def __init__(self, kind, base, size):
             side = size // 2
             self.side, self.eighth = side, side // 8
             self.ours, self.theirs = rows_at(base + core * side, side), rows_at(base + (1 - core) * side, side)
             self.own = rows_at(base + core * side + x * (2 * self.eighth), 2 * self.eighth)
             self.ring = Ring(
-                copies, x, x_after, x_before, base + core * side, 2 * self.eighth, self.eighth, self.eighth
+                copies, x, x_after, x_before, x_across, base + core * side, 2 * self.eighth, self.eighth, self.eighth
             )
-            self.steps = [
-                self.pair_first,
-                self.pair_then_ring,
-                self.ring_second,
-                self.ring_then_across,
-                self.across_then_gather,
-                self.gather_second,
-                self.gather_then_pair,
-                self.pair_end,
-            ]
+            reduce_kind, gather_kind = kind
+            self.steps = [self.pair_first, self.pair_then_ring]
+            if reduce_kind == "A":
+                self.reduce_first, self.reduce_last = self.ring.reduce_first, self.ring.reduce_last
+                self.steps.append(self.ring_second)
+            else:
+                self.reduce_first, self.reduce_last = self.ring.reduce_at_once, self.ring.reduce_at_once_last
+            self.steps += [self.ring_then_across, self.across_then_gather]
+            if gather_kind == "A":
+                self.gather_first, self.gather_rest = self.ring.gather_first, self.ring.gather_rest
+                self.steps.append(self.gather_second)
+            else:
+                self.gather_first, self.gather_rest = self.ring.gather_at_once, self.ring.gather_at_once_last
+            self.steps += [self.gather_then_pair, self.pair_end]
 
         def pair_first(self):
             self.pair = copies.group()
@@ -387,62 +424,60 @@
         def pair_then_ring(self):
             copies.arrived(self.pair, self.side)
             part_two[self.ours] = part_two[self.ours] + inbox[self.pair_room]
-            self.ring.reduce_first(part_two)
+            self.reduce_first(part_two)
 
         def ring_second(self):
             self.ring.reduce_second(part_two)
 
         def ring_then_across(self):
-            self.ring.reduce_last(part_two)
+            self.reduce_last(part_two)
             self.across = copies.group()
             self.across_room = copies.hand(part_two, self.own, 2 * self.eighth, z_across, self.across)
 
         def across_then_gather(self):
             copies.arrived(self.across, 2 * self.eighth)
             full_two[self.own] = part_two[self.own] + inbox[self.across_room]
-            self.ring.gather_first(full_two)
+            self.gather_first(full_two)
 
         def gather_second(self):
             self.ring.gather_second(full_two)
 
         def gather_then_pair(self):
-            self.ring.gather_near()
-            self.ring.gather_last()
+            self.gather_rest()
             self.back = copies.group()
             copies.push(full_two, self.ours, sibling, self.back)
 
         def pair_end(self):
             copies.arrived(self.back, self.side)
 
-    def run(chunks, order, places, scatter_block, gather_block, aside=None):
-        per_block = BLOCK // (atoms // len(chunks))
+    def run(chunks, order, places, scatter_block, gather_chunk, aside=None):
         done = [0] * len(chunks)
-        scattered, ended, gathered = set(), {}, 0
+        scattered, ended = set(), 0
         for i, k in enumerate(order):
             if i == len(chunks) and aside is not None:
                 aside()
-            block = places[k] // per_block
+            block = places[k] * CHUNK // BLOCK
             if block not in scattered:
                 scattered.add(block)
                 scatter_block(block)
             chunks[k].steps[done[k]]()
             done[k] += 1
             if done[k] == len(chunks[k].steps):
-                ended[block] = ended.get(block, 0) + 1
-                if ended[block] == per_block:
-                    gather_block(block, gathered == 0)
-                    gathered += 1
+                ended += 1
+                if ended == len(chunks):
+                    last = places[k]
+                else:
+                    gather_chunk(places[k], ended == 1)
         assert all(d == len(c.steps) for d, c in zip(done, chunks))
+        return last
 
     def scatter_one(block):
         scatter(part_one, state_ref, target_ref, block)
-        if block == PLACE_ONE[ORDER_ONE[0]] // (BLOCK * len(KINDS_ONE) // atoms):
+        if block == PLACE_ONE[ORDER_ONE[0]] * CHUNK // BLOCK:
             pl.semaphore_wait(barrier, len(partners))
 
-    size_one = atoms // len(KINDS_ONE)
-    chunks_one = [LayerOne(kind, place * size_one, size_one) for kind, place in zip(KINDS_ONE, PLACE_ONE)]
-    size_two = atoms // len(PLACE_TWO)
-    chunks_two = [LayerTwo(place * size_two, size_two) for place in PLACE_TWO]
+    chunks_one = [LayerOne(kind, place * CHUNK, CHUNK) for kind, place in zip(KINDS_ONE, PLACE_ONE)]
+    chunks_two = [LayerTwo(kind, place * CHUNK, CHUNK) for kind, place in zip(KINDS_TWO, PLACE_TWO)]
 
     def mark_both():
         for load in loads[3:]:
@@ -450,31 +485,40 @@
         mark(ones_one, target_ref)
         mark(ones_two, source_ref)
 
-    def gather_one(block, first):
-        gather(full_one, ones_one, block, state_ref, first)
-
-    run(chunks_one, ORDER_ONE, PLACE_ONE, scatter_one, gather_one, mark_both)
+    last = run(
+        chunks_one,
+        ORDER_ONE,
+        PLACE_ONE,
+        scatter_one,
+        lambda place, first: gather(full_one, ones_one, place, state_ref, first),
+        mark_both,
+    )
+    layer(full_one, ones_one, last, inner_one_ref, outer_one_ref, gain_one_ref, reverse)
     copies.all_sent()
     copies.send_sem, copies.sent = send_sems.at[1], 0
-    layer(inner_one_ref, outer_one_ref, gain_one_ref, reverse)
-
-    def gather_two(block, first):
-        gather(full_two, ones_two, block, reverse, first)
-
-    run(
+
+    last = run(
         chunks_two,
         ORDER_TWO,
         PLACE_TWO,
         lambda block: scatter(part_two, reverse, source_ref, block),
-        gather_two,
+        lambda place, first: gather(full_two, ones_two, place, reverse, first),
     )
-    layer(inner_two_ref, outer_two_ref, gain_two_ref, out_ref)
+    layer(full_two, ones_two, last, inner_two_ref, outer_two_ref, gain_two_ref, out_ref)
 
     copies.all_sent()
     assert copies.groups == GROUPS
 
 
-GROUPS = 8 * (len(KINDS_ONE) + len(PLACE_TWO))
+def groups_of(kind):
+    return 4 + (3 if kind[1] == "A" else 4)
+
+
+def groups_of_two(kind):
+    return 3 + (2 if kind[0] == "A" else 1) + (2 if kind[1] == "A" else 1)
+
+
+GROUPS = sum(map(groups_of, KINDS_ONE)) + sum(map(groups_of_two, KINDS_TWO))
 
 
 def body(
@@ -521,8 +565,7 @@
             pltpu.VMEM((atoms, channels), F32),
             pltpu.VMEM((rows, channels), F32),
             pltpu.VMEM((rows, channels), BF16),
-            pltpu.VMEM((BLOCK, channels), BF16),
-            pltpu.VMEM((BLOCK, channels), BF16),
+            pltpu.VMEM((2 * CHUNK, channels), BF16),
             pltpu.VMEM((rows, atoms), BF16),
             pltpu.VMEM((rows, atoms), BF16),
             pltpu.VMEM((2 * atoms, channels), F32),

time: 89.2 us -> 84.7 us (0.950)
  Pallas kernels: 86.2 us -> 81.7 us
    pallas_call x1, Pallas kernels: 86.2 us -> 81.7 us  [body(): pl.pallas_call(kernel, out_shape=jax.ShapeDtypeStruct((rows, channels), B...]
where the time goes in v3:
time: 84.7 us; the launch traced here: 84.6 us
  Pallas kernels  81.7 us (96%)
  local copies, waits for them, and re-layouts  2.26 us (3%)
    pallas_call x1, Pallas kernels, body(): pl.pallas_call(kernel, out_shape=jax.ShapeDtypeStruct((rows, channels), B...  81.7 us
    unnamed x1, local copies, waits for them, and re-layouts  2.26 us

profile of v3, /device:TPU:1, one launch (start us, length us, event | category | flops | bytes accessed | tf_op | source)
XLA Modules:
  0.0 84.6 jit_solution(1558144546956396726)
XLA Ops:
  0.7 81.7 %shard_map.100 = bf16[1024,512]{1,0:T(8,128)(2,1)} custom-call(bf16[1024,512]{1,0:T(8,128)(2,1)} %bitcast.7, s32[1,1024]{1,0:T(1,128)} %bitcast.8, s32[1,1024]{1,0:T(1,128)} %bitcast.9, s32[1,1]{1,0:T(1,128)S(6)} %copy.12.live_hbm, bf16[512,512]{1,0:T(8,128)(2,1)} %inner_one_hbm.1, bf16[512,512]{1,0:T(8,128)(2,1)} %outer_one_hbm.1, ...), custom_call_target="tpu_custom_call" | custom-call | tf_op jit(solution)/shard_map/pallas_call | solution.py:555
  82.4 2.3 %copy.13 = bf16[1,1,1024,512]{3,2,1,0:T(8,128)(2,1)} copy(bf16[1,1,1024,512]{3,2,1,0:T(8,128)(2,1)} %bitcast.6) | data formatting | bytes 2097152

commit v4 on v3

--- a/solution.py
+++ b/solution.py
@@ -18,10 +18,10 @@
 
 KINDS_ONE = ('BA', 'AA', 'AA', 'BB', 'AB', 'AA', 'BA', 'AB')
 KINDS_TWO = ('aA', 'aa', 'aa', 'aA', 'aa', 'aa', 'aa', 'aa')
-ORDER_ONE = (6, 5, 7, 0, 5, 4, 7, 6, 5, 2, 3, 4, 6, 7, 0, 2, 5, 1, 4, 6, 0, 3, 7, 1, 2, 4, 5, 0, 3, 1, 6, 2, 7, 3, 5, 4, 1, 6, 7, 0, 2, 7, 5, 4, 3, 6, 1, 0, 7, 4, 3, 2, 4, 5, 1, 3, 0, 3, 2, 6, 7, 1, 4, 0, 3, 2, 1)
-ORDER_TWO = (3, 1, 0, 6, 3, 7, 6, 1, 2, 5, 0, 2, 3, 4, 6, 5, 4, 1, 0, 7, 2, 3, 5, 6, 4, 1, 7, 3, 0, 2, 5, 1, 0, 4, 1, 6, 7, 2, 5, 6, 3, 2, 5, 4, 3, 0, 7, 4, 0, 7)
-PLACE_ONE = (4, 7, 6, 5, 3, 0, 1, 2)
-PLACE_TWO = (6, 0, 2, 4, 5, 3, 1, 7)
+ORDER_ONE = (6, 5, 7, 0, 5, 4, 7, 6, 5, 2, 3, 4, 6, 7, 0, 2, 5, 1, 4, 6, 0, 3, 7, 1, 2, 4, 5, 0, 3, 1, 6, 2, 7, 3, 5, 4, 1, 6, 7, 0, 2, 7, 5, 4, 3, 6, 1, 0, 7, 4, 3, 2, 4, 5, 5, 1, 3, 0, 3, 2, 6, 6, 7, 7, 1, 4, 4, 0, 0, 3, 3, 2, 2, 1, 1)
+ORDER_TWO = (3, 1, 0, 6, 3, 7, 6, 1, 2, 5, 0, 2, 3, 4, 6, 5, 4, 1, 0, 7, 2, 3, 5, 6, 4, 1, 7, 3, 0, 2, 5, 1, 0, 4, 1, 1, 6, 7, 2, 5, 6, 6, 3, 2, 2, 5, 5, 4, 3, 3, 0, 7, 4, 4, 0, 0, 7, 7)
+PLACE_ONE = (3, 7, 5, 6, 4, 1, 0, 2)
+PLACE_TWO = (2, 1, 5, 0, 7, 6, 3, 4)
 
 
 class Copies:
@@ -164,7 +164,7 @@
     outer_two_hbm,
     gain_one_hbm,
     gain_two_hbm,
-    out_ref,
+    out_hbm,
     state_ref,
     source_ref,
     target_ref,
@@ -181,6 +181,7 @@
     full_two,
     message,
     reverse,
+    final,
     terms,
     ones_one,
     ones_two,
@@ -275,7 +276,7 @@
             else:
                 message[tile] = message[tile] + total
 
-    def layer(full, ones_ref, place, inner_ref, outer_ref, gain_ref, result_ref):
+    def layer(full, ones_ref, place, inner_ref, outer_ref, gain_ref, result_ref, after_tile=None):
         split(full, place)
         for t in range(rows // TILE):
             tile = pl.ds(t * TILE, TILE)
@@ -287,6 +288,8 @@
             result = normed + jnp.dot(activated, outer_ref[...], preferred_element_type=F32)
             keep = lax.broadcasted_iota(jnp.int32, (TILE, channels), 0) + t * TILE < live
             result_ref[tile] = jnp.where(keep, result, F32(0)).astype(BF16)
+            if after_tile is not None:
+                after_tile(tile, t)
 
     copies = Copies(inbox, send_sems.at[0], recv_sems)
 
@@ -452,7 +455,8 @@
 
     def run(chunks, order, places, scatter_block, gather_chunk, aside=None):
         done = [0] * len(chunks)
-        scattered, ended = set(), 0
+        scattered = set()
+        gathered = 0
         for i, k in enumerate(order):
             if i == len(chunks) and aside is not None:
                 aside()
@@ -460,16 +464,14 @@
             if block not in scattered:
                 scattered.add(block)
                 scatter_block(block)
-            chunks[k].steps[done[k]]()
+            if done[k] < len(chunks[k].steps):
+                chunks[k].steps[done[k]]()
+            elif i < len(order) - 1:
+                gather_chunk(places[k], gathered == 0)
+                gathered += 1
             done[k] += 1
-            if done[k] == len(chunks[k].steps):
-                ended += 1
-                if ended == len(chunks):
-                    last = places[k]
-                else:
-                    gather_chunk(places[k], ended == 1)
-        assert all(d == len(c.steps) for d, c in zip(done, chunks))
-        return last
+        assert all(d == len(c.steps) + 1 for d, c in zip(done, chunks))
+        return places[order[-1]]
 
     def scatter_one(block):
         scatter(part_one, state_ref, target_ref, block)
@@ -504,9 +506,18 @@
         lambda block: scatter(part_two, reverse, source_ref, block),
         lambda place, first: gather(full_two, ones_two, place, reverse, first),
     )
-    layer(full_two, ones_two, last, inner_two_ref, outer_two_ref, gain_two_ref, out_ref)
+
+    stores = []
+
+    def store(tile, t):
+        stores.append(pltpu.make_async_copy(final.at[tile], out_hbm.at[tile], local_sems.at[t]))
+        stores[-1].start()
+
+    layer(full_two, ones_two, last, inner_two_ref, outer_two_ref, gain_two_ref, final, store)
 
     copies.all_sent()
+    for copy in stores:
+        copy.wait()
     assert copies.groups == GROUPS
 
 
@@ -556,7 +567,7 @@
         kernel,
         out_shape=jax.ShapeDtypeStruct((rows, channels), BF16),
         in_specs=[pl.BlockSpec(memory_space=pltpu.HBM)] * len(operands),
-        out_specs=pl.BlockSpec(memory_space=pltpu.VMEM),
+        out_specs=pl.BlockSpec(memory_space=pltpu.HBM),
         scratch_shapes=[copy_of(i, operand) for i, operand in enumerate(operands)]
         + [
             pltpu.VMEM((atoms, channels), F32),
@@ -564,6 +575,7 @@
             pltpu.VMEM((atoms, channels), F32),
             pltpu.VMEM((atoms, channels), F32),
             pltpu.VMEM((rows, channels), F32),
+            pltpu.VMEM((rows, channels), BF16),
             pltpu.VMEM((rows, channels), BF16),
             pltpu.VMEM((2 * CHUNK, channels), BF16),
             pltpu.VMEM((rows, atoms), BF16),

time: 84.7 us -> 84 us (level)
  no operation moved by 1% of the time
where the time goes in v4:
time: 84 us; the launch traced here: 83.9 us
  Pallas kernels  81 us (96%)
  local copies, waits for them, and re-layouts  2.26 us (3%)
    pallas_call x1, Pallas kernels, body(): pl.pallas_call(kernel, out_shape=jax.ShapeDtypeStruct((rows, channels), B...  81 us
    unnamed x1, local copies, waits for them, and re-layouts  2.26 us

profile of v4, /device:TPU:1, one launch (start us, length us, event | category | flops | bytes accessed | tf_op | source)
XLA Modules:
  0.0 83.9 jit_solution(3497663753704568750)
XLA Ops:
  0.7 81.0 %shard_map.100 = bf16[1024,512]{1,0:T(8,128)(2,1)} custom-call(bf16[1024,512]{1,0:T(8,128)(2,1)} %bitcast.7, s32[1,1024]{1,0:T(1,128)} %bitcast.8, s32[1,1024]{1,0:T(1,128)} %bitcast.9, s32[1,1]{1,0:T(1,128)S(6)} %copy.12.live_hbm, bf16[512,512]{1,0:T(8,128)(2,1)} %inner_one_hbm.1, bf16[512,512]{1,0:T(8,128)(2,1)} %outer_one_hbm.1, ...), custom_call_target="tpu_custom_call" | custom-call | tf_op jit(solution)/shard_map/pallas_call | solution.py:566
  81.6 2.3 %copy.13 = bf16[1,1,1024,512]{3,2,1,0:T(8,128)(2,1)} copy(bf16[1,1,1024,512]{3,2,1,0:T(8,128)(2,1)} %bitcast.6) | data formatting | bytes 2097152

commit v5 on v4

--- a/solution.py
+++ b/solution.py
@@ -10,18 +10,39 @@
 MESH = pl.DeviceIdType.MESH
 RING = 4
 TILE = 512
-CHUNK = 128
+PART = 128
 BLOCK = 256
 LANES = 128
 BF16 = jnp.bfloat16
 F32 = jnp.float32
 
-KINDS_ONE = ('BA', 'AA', 'AA', 'BB', 'AB', 'AA', 'BA', 'AB')
-KINDS_TWO = ('aA', 'aa', 'aa', 'aA', 'aa', 'aa', 'aa', 'aa')
-ORDER_ONE = (6, 5, 7, 0, 5, 4, 7, 6, 5, 2, 3, 4, 6, 7, 0, 2, 5, 1, 4, 6, 0, 3, 7, 1, 2, 4, 5, 0, 3, 1, 6, 2, 7, 3, 5, 4, 1, 6, 7, 0, 2, 7, 5, 4, 3, 6, 1, 0, 7, 4, 3, 2, 4, 5, 5, 1, 3, 0, 3, 2, 6, 6, 7, 7, 1, 4, 4, 0, 0, 3, 3, 2, 2, 1, 1)
-ORDER_TWO = (3, 1, 0, 6, 3, 7, 6, 1, 2, 5, 0, 2, 3, 4, 6, 5, 4, 1, 0, 7, 2, 3, 5, 6, 4, 1, 7, 3, 0, 2, 5, 1, 0, 4, 1, 1, 6, 7, 2, 5, 6, 6, 3, 2, 2, 5, 5, 4, 3, 3, 0, 7, 4, 4, 0, 0, 7, 7)
-PLACE_ONE = (3, 7, 5, 6, 4, 1, 0, 2)
-PLACE_TWO = (2, 1, 5, 0, 7, 6, 3, 4)
+CHUNKS_ONE = (
+    ("A", "A", 128, 256),
+    ("b", "A", 64, 64),
+    ("b", "b", 64, 512),
+    ("A", "b", 64, 576),
+    ("A", "A", 64, 448),
+    ("b", "A", 64, 0),
+    ("b", "A", 64, 768),
+    ("A", "B", 128, 640),
+    ("b", "A", 64, 384),
+    ("A", "b", 64, 832),
+    ("A", "A", 128, 896),
+    ("a", "a", 64, 128),
+    ("b", "b", 64, 192),
+)
+CHUNKS_TWO = (
+    ("a", "A", 128, 256),
+    ("a", "a", 128, 128),
+    ("a", "a", 128, 640),
+    ("a", "A", 128, 0),
+    ("a", "a", 128, 896),
+    ("a", "a", 128, 768),
+    ("a", "a", 128, 384),
+    ("a", "a", 128, 512),
+)
+ORDER_ONE = (1, 11, 0, 5, 4, 12, 2, 7, 11, 0, 8, 1, 5, 4, 6, 12, 7, 10, 0, 11, 2, 1, 4, 5, 3, 9, 12, 7, 0, 10, 8, 11, 4, 1, 6, 2, 5, 3, 7, 9, 10, 12, 11, 8, 0, 3, 6, 1, 9, 4, 5, 10, 2, 7, 0, 3, 8, 5, 9, 12, 4, 6, 2, 7, 1, 0, 10, 2, 8, 7, 12, 3, 5, 9, 6, 1, 7, 11, 10, 0, 3, 8, 4, 3, 9, 6, 9, 12, 2, 10, 7, 3, 8, 4, 6, 9, 10)
+ORDER_TWO = (3, 1, 0, 6, 3, 7, 6, 1, 2, 5, 0, 2, 3, 4, 6, 5, 4, 1, 0, 7, 2, 3, 5, 6, 4, 1, 7, 3, 0, 2, 5, 1, 0, 4, 1, 6, 7, 2, 5, 6, 3, 2, 5, 4, 3, 0, 7, 4, 0, 7)
 
 
 class Copies:
@@ -129,27 +150,38 @@
     def gather_rest(self):
         self.copies.arrived(self.near_group, 4 * self.count)
 
+
+class DirectRing(Ring):
     def shard(self, step):
         return rows_at(self.base + (self.me + step + RING) % RING * self.shard_stride, 2 * self.count)
 
-    def reduce_at_once(self, data):
+    def reduce_first(self, data):
         self.reduce_group = self.copies.group()
         self.terms = [
             self.copies.hand(data, self.shard(step), 2 * self.count, device, self.reduce_group)
             for step, device in ((1, self.after), (-1, self.before), (2, self.across))
         ]
 
-    def reduce_at_once_last(self, data):
+    def reduce_last(self, data):
         self.copies.arrived(self.reduce_group, 6 * self.count)
         rows, inbox = self.shard(0), self.copies.inbox
         data[rows] = data[rows] + inbox[self.terms[0]] + inbox[self.terms[1]] + inbox[self.terms[2]]
 
-    def gather_at_once(self, full):
+    def gather_first(self, full, apart=False):
         self.near_group = self.copies.group()
-        for device in (self.after, self.before, self.across):
-            self.copies.push(full, self.shard(0), device, self.near_group)
-
-    def gather_at_once_last(self):
+        self.last_group = self.copies.group() if apart else self.near_group
+        own = self.shard(0)
+        self.copies.push(full, own, self.after, self.near_group)
+        self.copies.push(full, own, self.before, self.near_group)
+        self.copies.push(full, own, self.across, self.last_group)
+
+    def gather_near(self):
+        self.copies.arrived(self.near_group, 4 * self.count)
+
+    def gather_last(self):
+        self.copies.arrived(self.last_group, 2 * self.count)
+
+    def gather_rest(self):
         self.copies.arrived(self.near_group, 6 * self.count)
 
 
@@ -197,6 +229,7 @@
     y, z_lo = src // 4, src % 4
     z_hi, x, core = tgt // 8, (tgt // 2) % 4, tgt % 2
     y_after, y_before = (((y + 1) % 4) * 4 + z_lo, tgt), (((y + 3) % 4) * 4 + z_lo, tgt)
+    y_across = (((y + 2) % 4) * 4 + z_lo, tgt)
     parity = z_lo % 2
     z_near, z_far = (y * 4 + z_lo + 1 - 2 * parity, tgt), (y * 4 + (z_lo + 2) % 4, tgt)
     sibling = (src, tgt + 1 - 2 * core)
@@ -206,7 +239,7 @@
     z_across = (src, (1 - z_hi) * 8 + x * 2 + core)
 
     barrier = pltpu.get_barrier_semaphore()
-    partners = (y_after, y_before, z_near, z_far, sibling, x_after, x_before, x_across, z_across)
+    partners = (y_after, y_before, y_across, z_near, z_far, sibling, x_after, x_before, x_across, z_across)
     for device in partners:
         pl.semaphore_signal(barrier, inc=1, device_id=device, device_id_type=MESH)
 
@@ -257,14 +290,14 @@
                 ).astype(BF16)
 
     def pick(full, ones_ref, place, t):
-        ones = ones_ref[pl.ds(t * TILE, TILE), pl.ds(place * CHUNK, CHUNK)]
+        ones = ones_ref[pl.ds(t * TILE, TILE), pl.ds(place * PART, PART)]
         return jnp.dot(jnp.concatenate([ones, ones], axis=1), terms[...], preferred_element_type=F32)
 
     def split(full, place):
-        values = full[pl.ds(place * CHUNK, CHUNK)]
+        values = full[pl.ds(place * PART, PART)]
         upper = values.astype(BF16)
-        terms[pl.ds(0, CHUNK)] = upper
-        terms[pl.ds(CHUNK, CHUNK)] = (values - upper.astype(F32)).astype(BF16)
+        terms[pl.ds(0, PART)] = upper
+        terms[pl.ds(PART, PART)] = (values - upper.astype(F32)).astype(BF16)
 
     def gather(full, ones_ref, place, values_ref, first):
         split(full, place)
@@ -293,32 +326,37 @@
 
     copies = Copies(inbox, send_sems.at[0], recv_sems)
 
+    def ring_of(kind):
+        return Ring if kind.isupper() else DirectRing
+
     class LayerOne:
-        def __init__(self, kind, base, size):
+        def __init__(self, reduce_kind, gather_kind, size, base):
             self.size = size
-            reduce_kind, gather_kind = kind
             eighth = size // 8
-            if reduce_kind == "A":
+            relayed = [self.ring_second] if reduce_kind.isupper() else []
+            if reduce_kind in "Aa":
                 shard_stride, part_stride = 2 * eighth, eighth
-                self.reduce_ring = self.ring(base, shard_stride, part_stride, eighth)
-                self.mine = rows_at(base + y * shard_stride + parity * part_stride, eighth)
-                self.theirs = rows_at(base + y * shard_stride + (1 - parity) * part_stride, eighth)
-                steps = [self.ring_first, self.ring_second, self.ring_then_near, self.near_then_far]
+                self.reduce_ring = self.ring(reduce_kind, base, shard_stride, part_stride, eighth)
+                steps = [self.ring_first, *relayed, self.ring_then_near, self.near_then_far]
             else:
                 shard_stride, part_stride = eighth, 4 * eighth
-                self.reduce_ring = self.ring(base + parity * part_stride, shard_stride, eighth // 2, eighth // 2)
-                self.mine = rows_at(base + y * shard_stride + parity * part_stride, eighth)
+                self.reduce_ring = self.ring(
+                    reduce_kind, base + parity * part_stride, shard_stride, eighth // 2, eighth // 2
+                )
                 self.upper = rows_at(base + parity * part_stride, part_stride)
                 self.lower = rows_at(base + (1 - parity) * part_stride, part_stride)
-                steps = [self.near_first, self.near_then_ring, self.ring_second, self.ring_then_far]
-            if gather_kind == "A":
-                self.gather_ring = self.ring(base, shard_stride, part_stride, eighth)
-                steps += [self.far_then_near, self.near_then_gather, self.gather_second, self.gather_end]
+                steps = [self.near_first, self.near_then_ring, *relayed, self.ring_then_far]
+            self.mine = rows_at(base + y * shard_stride + parity * part_stride, eighth)
+            self.theirs = rows_at(base + y * shard_stride + (1 - parity) * part_stride, eighth)
+            relayed = [self.gather_second] if gather_kind.isupper() else []
+            if gather_kind in "Aa":
+                self.gather_ring = self.ring(gather_kind, base, shard_stride, part_stride, eighth)
+                steps += [self.far_then_near, self.near_then_gather, *relayed, self.gather_end]
             else:
                 self.gather_ring = self.ring(
-                    base + parity * part_stride, shard_stride, eighth // 2, eighth // 2
+                    gather_kind, base + parity * part_stride, shard_stride, eighth // 2, eighth // 2
                 )
-                steps += [self.far_then_gather, self.gather_second, self.near_backs, self.last_backs, self.backs_end]
+                steps += [self.far_then_gather, *relayed, self.near_backs, self.last_backs, self.backs_end]
             self.steps = steps
 
             def shard(step):
@@ -326,8 +364,8 @@
 
             self.shard = shard
 
-        def ring(self, *where):
-            return Ring(copies, y, y_after, y_before, None, *where)
+        def ring(self, kind, *where):
+            return ring_of(kind)(copies, y, y_after, y_before, y_across, *where)
 
         def ring_first(self):
             self.reduce_ring.reduce_first(part_one)
@@ -397,27 +435,20 @@
             copies.arrived(self.back, self.size // 2)
 
     class LayerTwo:
-        def __init__(self, kind, base, size):
-            side = size // 2
-            self.side, self.eighth = side, side // 8
-            self.ours, self.theirs = rows_at(base + core * side, side), rows_at(base + (1 - core) * side, side)
-            self.own = rows_at(base + core * side + x * (2 * self.eighth), 2 * self.eighth)
-            self.ring = Ring(
-                copies, x, x_after, x_before, x_across, base + core * side, 2 * self.eighth, self.eighth, self.eighth
-            )
-            reduce_kind, gather_kind = kind
+        def __init__(self, reduce_kind, gather_kind, size, base):
+            side, eighth = size // 2, size // 16
+            base_here = base + core * side
+            self.side, self.shard = side, 2 * eighth
+            self.ours, self.theirs = rows_at(base_here, side), rows_at(base + (1 - core) * side, side)
+            self.own = rows_at(base_here + x * self.shard, self.shard)
+            self.reduce_ring, self.gather_ring = [
+                ring_of(kind)(copies, x, x_after, x_before, x_across, base_here, self.shard, eighth, eighth)
+                for kind in (reduce_kind, gather_kind)
+            ]
             self.steps = [self.pair_first, self.pair_then_ring]
-            if reduce_kind == "A":
-                self.reduce_first, self.reduce_last = self.ring.reduce_first, self.ring.reduce_last
-                self.steps.append(self.ring_second)
-            else:
-                self.reduce_first, self.reduce_last = self.ring.reduce_at_once, self.ring.reduce_at_once_last
+            self.steps += [self.ring_second] if reduce_kind.isupper() else []
             self.steps += [self.ring_then_across, self.across_then_gather]
-            if gather_kind == "A":
-                self.gather_first, self.gather_rest = self.ring.gather_first, self.ring.gather_rest
-                self.steps.append(self.gather_second)
-            else:
-                self.gather_first, self.gather_rest = self.ring.gather_at_once, self.ring.gather_at_once_last
+            self.steps += [self.gather_second] if gather_kind.isupper() else []
             self.steps += [self.gather_then_pair, self.pair_end]
 
         def pair_first(self):
@@ -427,59 +458,62 @@
         def pair_then_ring(self):
             copies.arrived(self.pair, self.side)
             part_two[self.ours] = part_two[self.ours] + inbox[self.pair_room]
-            self.reduce_first(part_two)
+            self.reduce_ring.reduce_first(part_two)
 
         def ring_second(self):
-            self.ring.reduce_second(part_two)
+            self.reduce_ring.reduce_second(part_two)
 
         def ring_then_across(self):
-            self.reduce_last(part_two)
+            self.reduce_ring.reduce_last(part_two)
             self.across = copies.group()
-            self.across_room = copies.hand(part_two, self.own, 2 * self.eighth, z_across, self.across)
+            self.across_room = copies.hand(part_two, self.own, self.shard, z_across, self.across)
 
         def across_then_gather(self):
-            copies.arrived(self.across, 2 * self.eighth)
+            copies.arrived(self.across, self.shard)
             full_two[self.own] = part_two[self.own] + inbox[self.across_room]
-            self.gather_first(full_two)
+            self.gather_ring.gather_first(full_two)
 
         def gather_second(self):
-            self.ring.gather_second(full_two)
+            self.gather_ring.gather_second(full_two)
 
         def gather_then_pair(self):
-            self.gather_rest()
+            self.gather_ring.gather_rest()
             self.back = copies.group()
             copies.push(full_two, self.ours, sibling, self.back)
 
         def pair_end(self):
             copies.arrived(self.back, self.side)
 
-    def run(chunks, order, places, scatter_block, gather_chunk, aside=None):
+    def run(layer_of, chunks, order, scatter_block, gather_part, aside=None):
+        made = [layer_of(*chunk) for chunk in chunks]
+        sizes, bases = [chunk[2] for chunk in chunks], [chunk[3] for chunk in chunks]
+        assert sum(sizes) == atoms
         done = [0] * len(chunks)
-        scattered = set()
-        gathered = 0
+        scattered, filled, gathered = set(), {}, 0
         for i, k in enumerate(order):
             if i == len(chunks) and aside is not None:
                 aside()
-            block = places[k] * CHUNK // BLOCK
+            block, part = bases[k] // BLOCK, bases[k] // PART
             if block not in scattered:
                 scattered.add(block)
-                scatter_block(block)
-            if done[k] < len(chunks[k].steps):
-                chunks[k].steps[done[k]]()
-            elif i < len(order) - 1:
-                gather_chunk(places[k], gathered == 0)
-                gathered += 1
+                scatter_block(block, len(scattered) == 1)
+            made[k].steps[done[k]]()
             done[k] += 1
-        assert all(d == len(c.steps) + 1 for d, c in zip(done, chunks))
-        return places[order[-1]]
-
-    def scatter_one(block):
+            if done[k] == len(made[k].steps):
+                filled[part] = filled.get(part, 0) + sizes[k]
+                if filled[part] == PART:
+                    gathered += 1
+                    if gathered < atoms // PART:
+                        gather_part(part, gathered == 1)
+                    else:
+                        last = part
+        assert all(d == len(m.steps) for d, m in zip(done, made))
+        return last
+
+    def scatter_one(block, first):
         scatter(part_one, state_ref, target_ref, block)
-        if block == PLACE_ONE[ORDER_ONE[0]] * CHUNK // BLOCK:
+        if first:
             pl.semaphore_wait(barrier, len(partners))
-
-    chunks_one = [LayerOne(kind, place * CHUNK, CHUNK) for kind, place in zip(KINDS_ONE, PLACE_ONE)]
-    chunks_two = [LayerTwo(kind, place * CHUNK, CHUNK) for kind, place in zip(KINDS_TWO, PLACE_TWO)]
 
     def mark_both():
         for load in loads[3:]:
@@ -488,9 +522,9 @@
         mark(ones_two, source_ref)
 
     last = run(
-        chunks_one,
+        LayerOne,
+        CHUNKS_ONE,
         ORDER_ONE,
-        PLACE_ONE,
         scatter_one,
         lambda place, first: gather(full_one, ones_one, place, state_ref, first),
         mark_both,
@@ -500,10 +534,10 @@
     copies.send_sem, copies.sent = send_sems.at[1], 0
 
     last = run(
-        chunks_two,
+        LayerTwo,
+        CHUNKS_TWO,
         ORDER_TWO,
-        PLACE_TWO,
-        lambda block: scatter(part_two, reverse, source_ref, block),
+        lambda block, first: scatter(part_two, reverse, source_ref, block),
         lambda place, first: gather(full_two, ones_two, place, reverse, first),
     )
 
@@ -521,15 +555,11 @@
     assert copies.groups == GROUPS
 
 
-def groups_of(kind):
-    return 4 + (3 if kind[1] == "A" else 4)
-
-
-def groups_of_two(kind):
-    return 3 + (2 if kind[0] == "A" else 1) + (2 if kind[1] == "A" else 1)
-
-
-GROUPS = sum(map(groups_of, KINDS_ONE)) + sum(map(groups_of_two, KINDS_TWO))
+def groups_of(reduce_kind, gather_kind, *_):
+    return 5 + reduce_kind.isupper() + gather_kind.isupper() + (gather_kind in "Bb")
+
+
+GROUPS = sum(groups_of(*chunk) for chunk in CHUNKS_ONE + CHUNKS_TWO)
 
 
 def body(
@@ -577,7 +607,7 @@
             pltpu.VMEM((rows, channels), F32),
             pltpu.VMEM((rows, channels), BF16),
             pltpu.VMEM((rows, channels), BF16),
-            pltpu.VMEM((2 * CHUNK, channels), BF16),
+            pltpu.VMEM((2 * PART, channels), BF16),
             pltpu.VMEM((rows, atoms), BF16),
             pltpu.VMEM((rows, atoms), BF16),
             pltpu.VMEM((2 * atoms, channels), F32),

time: 84 us -> 82.3 us (0.980)
  Pallas kernels: 81 us -> 79.2 us
    pallas_call x1, Pallas kernels: 81 us -> 79.2 us  [body(): pl.pallas_call(kernel, out_shape=jax.ShapeDtypeStruct((rows, channels), B...]
where the time goes in v5:
time: 82.3 us; the launch traced here: 82.1 us
  Pallas kernels  79.2 us (96%)
  local copies, waits for them, and re-layouts  2.26 us (3%)
    pallas_call x1, Pallas kernels, body(): pl.pallas_call(kernel, out_shape=jax.ShapeDtypeStruct((rows, channels), B...  79.2 us
    unnamed x1, local copies, waits for them, and re-layouts  2.26 us

profile of v5, /device:TPU:1, one launch (start us, length us, event | category | flops | bytes accessed | tf_op | source)
XLA Modules:
  0.0 82.1 jit_solution(5341829502571497330)
XLA Ops:
  0.7 79.2 %shard_map.100 = bf16[1024,512]{1,0:T(8,128)(2,1)} custom-call(bf16[1024,512]{1,0:T(8,128)(2,1)} %bitcast.7, s32[1,1024]{1,0:T(1,128)} %bitcast.8, s32[1,1024]{1,0:T(1,128)} %bitcast.9, s32[1,1]{1,0:T(1,128)S(6)} %copy.12.live_hbm, bf16[512,512]{1,0:T(8,128)(2,1)} %inner_one_hbm.1, bf16[512,512]{1,0:T(8,128)(2,1)} %outer_one_hbm.1, ...), custom_call_target="tpu_custom_call" | custom-call | tf_op jit(solution)/shard_map/pallas_call | solution.py:596
  79.9 2.3 %copy.13 = bf16[1,1,1024,512]{3,2,1,0:T(8,128)(2,1)} copy(bf16[1,1,1024,512]{3,2,1,0:T(8,128)(2,1)} %bitcast.6) | data formatting | bytes 2097152

commit v6 on v5

--- a/solution.py
+++ b/solution.py
@@ -17,19 +17,20 @@
 F32 = jnp.float32
 
 CHUNKS_ONE = (
-    ("A", "A", 128, 256),
+    ("A", "A", 64, 704),
+    ("b", "A", 64, 576),
+    ("A", "A", 64, 256),
+    ("A", "B", 128, 384),
     ("b", "A", 64, 64),
-    ("b", "b", 64, 512),
-    ("A", "b", 64, 576),
-    ("A", "A", 64, 448),
-    ("b", "A", 64, 0),
-    ("b", "A", 64, 768),
-    ("A", "B", 128, 640),
-    ("b", "A", 64, 384),
-    ("A", "b", 64, 832),
-    ("A", "A", 128, 896),
-    ("a", "a", 64, 128),
-    ("b", "b", 64, 192),
+    ("B", "B", 128, 768),
+    ("A", "b", 64, 320),
+    ("A", "b", 64, 192),
+    ("b", "A", 64, 128),
+    ("A", "a", 64, 960),
+    ("A", "A", 64, 640),
+    ("a", "a", 64, 0),
+    ("b", "A", 64, 512),
+    ("a", "b", 64, 896),
 )
 CHUNKS_TWO = (
     ("a", "A", 128, 256),
@@ -41,7 +42,7 @@
     ("a", "a", 128, 384),
     ("a", "a", 128, 512),
 )
-ORDER_ONE = (1, 11, 0, 5, 4, 12, 2, 7, 11, 0, 8, 1, 5, 4, 6, 12, 7, 10, 0, 11, 2, 1, 4, 5, 3, 9, 12, 7, 0, 10, 8, 11, 4, 1, 6, 2, 5, 3, 7, 9, 10, 12, 11, 8, 0, 3, 6, 1, 9, 4, 5, 10, 2, 7, 0, 3, 8, 5, 9, 12, 4, 6, 2, 7, 1, 0, 10, 2, 8, 7, 12, 3, 5, 9, 6, 1, 7, 11, 10, 0, 3, 8, 4, 3, 9, 6, 9, 12, 2, 10, 7, 3, 8, 4, 6, 9, 10)
+ORDER_ONE = (11, 8, 2, 3, 7, 1, 4, 10, 0, 12, 11, 8, 2, 5, 3, 4, 7, 10, 1, 0, 11, 2, 8, 9, 3, 6, 12, 4, 7, 10, 5, 0, 2, 9, 1, 11, 6, 3, 13, 8, 7, 10, 5, 4, 9, 6, 11, 0, 12, 2, 1, 8, 5, 13, 4, 3, 6, 9, 7, 10, 2, 1, 8, 0, 12, 13, 3, 3, 4, 5, 6, 10, 9, 7, 0, 12, 7, 11, 13, 3, 4, 6, 2, 5, 10, 1, 5, 6, 0, 8, 12, 9, 7, 13, 13, 5, 10, 3, 0, 2, 6, 12, 1, 13, 9, 5)
 ORDER_TWO = (3, 1, 0, 6, 3, 7, 6, 1, 2, 5, 0, 2, 3, 4, 6, 5, 4, 1, 0, 7, 2, 3, 5, 6, 4, 1, 7, 3, 0, 2, 5, 1, 0, 4, 1, 6, 7, 2, 5, 6, 3, 2, 5, 4, 3, 0, 7, 4, 0, 7)
 
 

time: 82.3 us -> 81.7 us (level)
  no operation moved by 1% of the time
where the time goes in v6:
time: 81.7 us; the launch traced here: 81.5 us
  Pallas kernels  78.6 us (96%)
  local copies, waits for them, and re-layouts  2.26 us (3%)
    pallas_call x1, Pallas kernels, body(): pl.pallas_call(kernel, out_shape=jax.ShapeDtypeStruct((rows, channels), B...  78.6 us
    unnamed x1, local copies, waits for them, and re-layouts  2.26 us

profile of v6, /device:TPU:1, one launch (start us, length us, event | category | flops | bytes accessed | tf_op | source)
XLA Modules:
  0.0 81.5 jit_solution(7110578048483585144)
XLA Ops:
  0.7 78.6 %shard_map.100 = bf16[1024,512]{1,0:T(8,128)(2,1)} custom-call(bf16[1024,512]{1,0:T(8,128)(2,1)} %bitcast.7, s32[1,1024]{1,0:T(1,128)} %bitcast.8, s32[1,1024]{1,0:T(1,128)} %bitcast.9, s32[1,1]{1,0:T(1,128)S(6)} %copy.12.live_hbm, bf16[512,512]{1,0:T(8,128)(2,1)} %inner_one_hbm.1, bf16[512,512]{1,0:T(8,128)(2,1)} %outer_one_hbm.1, ...), custom_call_target="tpu_custom_call" | custom-call | tf_op jit(solution)/shard_map/pallas_call | solution.py:597
  79.3 2.3 %copy.13 = bf16[1,1,1024,512]{3,2,1,0:T(8,128)(2,1)} copy(bf16[1,1,1024,512]{3,2,1,0:T(8,128)(2,1)} %bitcast.6) | data formatting | bytes 2097152

commit v7 on v6

--- a/solution.py
+++ b/solution.py
@@ -320,9 +320,11 @@
             activated = jnp.dot(normed.astype(BF16), inner_ref[...], preferred_element_type=F32)
             activated = jnp.maximum(activated, F32(0)).astype(BF16)
             result = normed + jnp.dot(activated, outer_ref[...], preferred_element_type=F32)
-            keep = lax.broadcasted_iota(jnp.int32, (TILE, channels), 0) + t * TILE < live
-            result_ref[tile] = jnp.where(keep, result, F32(0)).astype(BF16)
-            if after_tile is not None:
+            if after_tile is None:
+                result_ref[tile] = result.astype(BF16)
+            else:
+                keep = lax.broadcasted_iota(jnp.int32, (TILE, channels), 0) + t * TILE < live
+                result_ref[tile] = jnp.where(keep, result, F32(0)).astype(BF16)
                 after_tile(tile, t)
 
     copies = Copies(inbox, send_sems.at[0], recv_sems)

time: 81.7 us -> 81.6 us (level)
  no operation moved by 1% of the time
where the time goes in v7:
time: 81.6 us; the launch traced here: 81.5 us
  Pallas kernels  78.5 us (96%)
  local copies, waits for them, and re-layouts  2.26 us (3%)
    pallas_call x1, Pallas kernels, body(): pl.pallas_call(kernel, out_shape=jax.ShapeDtypeStruct((rows, channels), B...  78.5 us
    unnamed x1, local copies, waits for them, and re-layouts  2.26 us

profile of v7, /device:TPU:1, one launch (start us, length us, event | category | flops | bytes accessed | tf_op | source)
XLA Modules:
  0.0 81.5 jit_solution(16300519605246080989)
XLA Ops:
  0.7 78.5 %shard_map.100 = bf16[1024,512]{1,0:T(8,128)(2,1)} custom-call(bf16[1024,512]{1,0:T(8,128)(2,1)} %bitcast.7, s32[1,1024]{1,0:T(1,128)} %bitcast.8, s32[1,1024]{1,0:T(1,128)} %bitcast.9, s32[1,1]{1,0:T(1,128)S(6)} %copy.12.live_hbm, bf16[512,512]{1,0:T(8,128)(2,1)} %inner_one_hbm.1, bf16[512,512]{1,0:T(8,128)(2,1)} %outer_one_hbm.1, ...), custom_call_target="tpu_custom_call" | custom-call | tf_op jit(solution)/shard_map/pallas_call | solution.py:599
  79.2 2.3 %copy.13 = bf16[1,1,1024,512]{3,2,1,0:T(8,128)(2,1)} copy(bf16[1,1,1024,512]{3,2,1,0:T(8,128)(2,1)} %bitcast.6) | data formatting | bytes 2097152
